TPU v7x, 256 devices: a whole 4x4x8 slice. The times are simulated.
256 devices in a mesh: island: 32 (over z_lo, y, core), fsdp: 8 (over x, z_hi).
Axes of the slice: x: 4, y: 4, z: 8 (z_hi: 2, z_lo: 4; z = z_hi * 4 + z_lo), core: 2. Of those that a mesh axis runs over, the one named last changes fastest.
Arguments:
- queries: bfloat16 [32, 2048, 2048], P('island', 'fsdp'), may hold values from -5 to 5
- keys: bfloat16 [32, 2048, 512], P('island', 'fsdp'), may hold values from -5 to 5
- values: bfloat16 [32, 2048, 512], P('island', 'fsdp'), may hold values from -6 to 6
- d_out: bfloat16 [32, 2048, 2048], P('island', 'fsdp'), may hold values from -6 to 6
- lengths: int32 [32], P('island'), may hold values from 256 to 2048
- steps: int32 [32], P('island'), may hold values from 50 to 100
- theta_global: float32 [768, 4096], P('fsdp'), may hold values from -6 to 6
- theta_local: bfloat16 [32, 768, 4096], P('island', 'fsdp'), may hold values from -6 to 6
- momentum: float32 [768, 4096], P('fsdp'), may hold values from -3 to 3
Outputs:
- context: bfloat16 [32, 2048, 2048], P('island', 'fsdp')
- d_queries: bfloat16 [32, 2048, 2048], P('island', 'fsdp')
- d_keys: bfloat16 [32, 2048, 512], P('island', 'fsdp')
- d_values: bfloat16 [32, 2048, 512], P('island', 'fsdp')
- theta_new: float32 [768, 4096], P('fsdp')
- momentum_new: float32 [768, 4096], P('fsdp')
All inputs are finite; a program needn't handle non-finite values.
Results may differ from a plain program's by a relative error of at most 0.0033.
The roundings to bfloat16 on the way count: a program that leaves them out, or rounds other values in their place, can miss the bound.
Values may be sent and summed in bfloat16 or wider, within the bound.
No kernel may reach another device: no remote copies, remote signals or barrier semaphores. Data moves between devices by JAX's collectives and lax.ppermute only.
A program may use at most 192 MiB of HBM per device.

v0:
```python
import jax
import jax.numpy as jnp
from jax import lax
from jax.sharding import PartitionSpec as P

QUERY_HEADS = 16
KEY_VALUE_HEADS = 4
HEAD_SIZE = 128


neg_large = -1e30
outer_momentum = 0.9
outer_rate = 0.7


def body(queries, keys, values, d_out, lengths, steps, theta_global, theta_local, momentum):
    token_list = queries.shape[1]
    key_width = keys.shape[2]
    group_width = QUERY_HEADS // KEY_VALUE_HEADS
    score_scale = HEAD_SIZE ** (-0.5)
    length = lengths[0]
    every_key, every_value = (
        lax.all_gather(keys, "fsdp", axis=1, tiled=True),
        lax.all_gather(values, "fsdp", axis=1, tiled=True),
    )
    window_extent = every_key.shape[1]
    query_pos = lax.axis_index("fsdp") * token_list + jnp.arange(token_list, dtype=jnp.int32)
    key_pos = jnp.arange(window_extent, dtype=jnp.int32)
    allowed = (key_pos[None, :] <= query_pos[:, None]) & (key_pos[None, :] < length)
    live = (query_pos < length)[:, None]
    output_masked = jnp.where(live, d_out[0], jnp.zeros_like(d_out[0]))
    query_head_rows = queries[0].reshape(token_list, KEY_VALUE_HEADS, group_width, HEAD_SIZE)
    head_masked = output_masked.reshape(token_list, KEY_VALUE_HEADS, group_width, HEAD_SIZE)
    key_head_rows = every_key[0].reshape(window_extent, KEY_VALUE_HEADS, HEAD_SIZE)
    value_head_rows = every_value[0].reshape(window_extent, KEY_VALUE_HEADS, HEAD_SIZE)

    def group_pass(operands):
        query_group, masked_group, key_group, value_group = operands
        scores = (
            jnp.einsum("qgd,kd->gqk", query_group, key_group, preferred_element_type=jnp.float32)
            * score_scale
        )
        scores = jnp.where(allowed, scores, neg_large)
        row_max = jnp.max(scores, axis=2, keepdims=True)
        total_group = row_max + jnp.log(jnp.sum(jnp.exp(scores - row_max), axis=2, keepdims=True))
        soft_weights = jnp.exp(scores - total_group)
        soft_group = soft_weights.astype(jnp.bfloat16)
        context_group = jnp.einsum(
            "gqk,kd->qgd", soft_group, value_group, preferred_element_type=jnp.float32
        )
        dots_group = jnp.transpose(
            jnp.sum(masked_group.astype(jnp.float32) * context_group, axis=2), (1, 0)
        )[..., None]
        prob_grad = jnp.einsum(
            "qgd,kd->gqk", masked_group, value_group, preferred_element_type=jnp.float32
        )
        grad_group = (soft_weights * (prob_grad - dots_group)).astype(jnp.bfloat16)
        qgrad_group = (
            jnp.einsum("gqk,kd->qgd", grad_group, key_group, preferred_element_type=jnp.float32)
            * score_scale
        )
        return (soft_group, grad_group, context_group, total_group, dots_group, qgrad_group)

    soft_rounded, grad_rounded, context_groups, log_total, row_dots, qgrad_groups = lax.map(
        group_pass,
        (
            jnp.transpose(query_head_rows, (1, 0, 2, 3)),
            jnp.transpose(head_masked, (1, 0, 2, 3)),
            jnp.transpose(key_head_rows, (1, 0, 2)),
            jnp.transpose(value_head_rows, (1, 0, 2)),
        ),
    )
    context = (
        jnp.transpose(context_groups, (1, 0, 2, 3))
        .astype(jnp.bfloat16)
        .reshape(1, token_list, QUERY_HEADS * HEAD_SIZE)
    )
    d_queries = (
        jnp.transpose(qgrad_groups, (1, 0, 2, 3))
        .astype(jnp.bfloat16)
        .reshape(1, token_list, QUERY_HEADS * HEAD_SIZE)
    )
    key_part = (
        jnp.einsum(
            "cgqk,qcgd->kcd", grad_rounded, query_head_rows, preferred_element_type=jnp.float32
        )
        * score_scale
    )
    value_part = jnp.einsum(
        "cgqk,qcgd->kcd", soft_rounded, head_masked, preferred_element_type=jnp.float32
    )
    summed = lax.psum_scatter(
        jnp.concatenate(
            (
                key_part.reshape(lax.axis_size("fsdp") * token_list, key_width),
                value_part.reshape(lax.axis_size("fsdp") * token_list, key_width),
            ),
            axis=1,
        ),
        "fsdp",
        scatter_dimension=0,
        tiled=True,
    )
    d_keys = summed[:, :key_width].astype(jnp.bfloat16)[None]
    d_values = summed[:, key_width:].astype(jnp.bfloat16)[None]
    weight = steps.astype(jnp.float32) * lengths.astype(jnp.float32)
    drift_terms = weight[0] * (theta_global - theta_local[0].astype(jnp.float32))
    weighted_sum, total_weight = lax.psum((drift_terms, weight), "island")
    pseudo = weighted_sum / total_weight[0]
    momentum_new = outer_momentum * momentum + pseudo
    theta_new = theta_global - outer_rate * (pseudo + outer_momentum * momentum_new)
    return (context, d_queries, d_keys, d_values, theta_new, momentum_new)


def solution(mesh):
    return jax.shard_map(
        body,
        mesh=mesh,
        in_specs=(
            P("island", "fsdp", None),
            P("island", "fsdp", None),
            P("island", "fsdp", None),
            P("island", "fsdp", None),
            P("island"),
            P("island"),
            P("fsdp", None),
            P("island", "fsdp", None),
            P("fsdp", None),
        ),
        out_specs=(
            P("island", "fsdp", None),
            P("island", "fsdp", None),
            P("island", "fsdp", None),
            P("island", "fsdp", None),
            P("fsdp", None),
            P("fsdp", None),
        ),
        check_vma=False,
    )
```

profile of v0, /device:TPU:16, one launch (start us, length us, event | category | flops | bytes accessed | tf_op | source)
XLA Modules:
  0.0 508.2 jit_solution(2585922312429527109)
XLA Ops:
  13.2 2.9 fusion.28
  19.2 72.2 %all-gather.3.cloned.1.call-done = bf16[1,2048,512]{1,2,0:T(8,128)(2,1)} async-done(((bf16[1,256,512]{1,2,0:T(8,128)(2,1)}), bf16[1,2048,512]{1,2,0:T(8,128)(2,1)}) %all-gather.3.cloned.1.call-update) | async-done | bytes 2097168 | tf_op jit(solution)/shard_map/all_gather | solution.py:23
  91.4 75.8 %all-gather.5.cloned.1.call-done = bf16[1,2048,512]{1,2,0:T(8,128)(2,1)} async-done(((bf16[1,256,512]{1,2,0:T(8,128)(2,1)}), bf16[1,2048,512]{1,2,0:T(8,128)(2,1)}) %all-gather.5.cloned.1.call-update) | async-done | bytes 2097168 | tf_op jit(solution)/shard_map/all_gather | solution.py:24
  167.2 105.0 %while.17 = (s32[]{:T(128)}, bf16[4,4,256,2048]{2,3,1,0:T(8,128)(2,1)}, bf16[4,4,256,2048]{2,3,1,0:T(8,128)(2,1)}, bf16[4,256,4,128]{3,1,2,0:T(8,128)(2,1)}, bf1...) while((s32[]{:T(128)}, ...), condition=%wide.region_4.5_spmd.clone, body=%wide.region_0.4_spmd.clone.sunk | while | flops 2193225728 | bytes 142659824 | solution.py:64
  167.6 2.6 fusion.46
  170.3 3.2 copy-done
  175.5 6.4 %fusion.47 = (f32[256,4]{0,1:T(4,128)S(1)}, bf16[128,4,256]{0,2,1:T(8,128)(2,1)S(1)}) fusion(bf16[1,256,4,128]{3,1,2,0:T(8,128)(2,1)S(1)} %copy.66, f32[2048,256,4]{1,0,2:T(8,128)} %copy-done, f32[4,256]{1,0:T(4,128)S(1)} %log_add_fusion.2, pred[256,2048]{0,1:T(8,128)(4,1)S(1)} %fusion.45, bf16[4,2048,128]{1,2,0:T(8,128)(2,1)} %get-tuple-element.257, ...), kind=kOutput, calls=%fused_computation.24.clone.1 | convolution fusion | flops 545782784 | bytes 9970176 | tf_op jit(solution)/shard_map/while/body/eval_jaxpr/gqk,kd->qgd/dot_general | solution.py:48
  182.0 5.7 %bitcast_dynamic-update-slice_fusion.7 = (bf16[4,4,256,2048]{2,3,1,0:T(8,128)(2,1)}, bf16[4,256,2048]{1,2,0:T(8,128)(2,1)S(1)}) fusion(bf16[4,4,256,2048]{2,3,1,0:T(8,128)(2,1)} %get-tuple-element.240, s32[]{:T(128)} %get-tuple-element.238, f32[4,256]{1,0:T(4,128)S(1)} %bitcast.168, bf16[4,256,4,128]{1,3,2,0:T(8,128)(2,1)S(1)} %get-tuple-element.258, ...), kind=kOutput, calls=%fused_computation.9.clone.1 | convolution fusion | flops 549453824 | bytes 18097664 | tf_op jit(solution)/shard_map/while/body/eval_jaxpr/qgd,kd->gqk/dot_general | solution.py:54
  189.4 3.3 bitcast_dynamic-update-slice_fusion.6
  193.9 2.6 fusion.46
  196.5 3.2 copy-done
  201.8 6.4 %fusion.47 = (f32[256,4]{0,1:T(4,128)S(1)}, bf16[128,4,256]{0,2,1:T(8,128)(2,1)S(1)}) fusion(bf16[1,256,4,128]{3,1,2,0:T(8,128)(2,1)S(1)} %copy.66, f32[2048,256,4]{1,0,2:T(8,128)} %copy-done, f32[4,256]{1,0:T(4,128)S(1)} %log_add_fusion.2, pred[256,2048]{0,1:T(8,128)(4,1)S(1)} %fusion.45, bf16[4,2048,128]{1,2,0:T(8,128)(2,1)} %get-tuple-element.257, ...), kind=kOutput, calls=%fused_computation.24.clone.1 | convolution fusion | flops 545782784 | bytes 9970176 | tf_op jit(solution)/shard_map/while/body/eval_jaxpr/gqk,kd->qgd/dot_general | solution.py:48
  208.2 5.7 %bitcast_dynamic-update-slice_fusion.7 = (bf16[4,4,256,2048]{2,3,1,0:T(8,128)(2,1)}, bf16[4,256,2048]{1,2,0:T(8,128)(2,1)S(1)}) fusion(bf16[4,4,256,2048]{2,3,1,0:T(8,128)(2,1)} %get-tuple-element.240, s32[]{:T(128)} %get-tuple-element.238, f32[4,256]{1,0:T(4,128)S(1)} %bitcast.168, bf16[4,256,4,128]{1,3,2,0:T(8,128)(2,1)S(1)} %get-tuple-element.258, ...), kind=kOutput, calls=%fused_computation.9.clone.1 | convolution fusion | flops 549453824 | bytes 18097664 | tf_op jit(solution)/shard_map/while/body/eval_jaxpr/qgd,kd->gqk/dot_general | solution.py:54
  215.7 3.3 bitcast_dynamic-update-slice_fusion.6
  220.1 2.6 fusion.46
  222.8 3.2 copy-done
  228.1 6.4 %fusion.47 = (f32[256,4]{0,1:T(4,128)S(1)}, bf16[128,4,256]{0,2,1:T(8,128)(2,1)S(1)}) fusion(bf16[1,256,4,128]{3,1,2,0:T(8,128)(2,1)S(1)} %copy.66, f32[2048,256,4]{1,0,2:T(8,128)} %copy-done, f32[4,256]{1,0:T(4,128)S(1)} %log_add_fusion.2, pred[256,2048]{0,1:T(8,128)(4,1)S(1)} %fusion.45, bf16[4,2048,128]{1,2,0:T(8,128)(2,1)} %get-tuple-element.257, ...), kind=kOutput, calls=%fused_computation.24.clone.1 | convolution fusion | flops 545782784 | bytes 9970176 | tf_op jit(solution)/shard_map/while/body/eval_jaxpr/gqk,kd->qgd/dot_general | solution.py:48
  234.5 5.7 %bitcast_dynamic-update-slice_fusion.7 = (bf16[4,4,256,2048]{2,3,1,0:T(8,128)(2,1)}, bf16[4,256,2048]{1,2,0:T(8,128)(2,1)S(1)}) fusion(bf16[4,4,256,2048]{2,3,1,0:T(8,128)(2,1)} %get-tuple-element.240, s32[]{:T(128)} %get-tuple-element.238, f32[4,256]{1,0:T(4,128)S(1)} %bitcast.168, bf16[4,256,4,128]{1,3,2,0:T(8,128)(2,1)S(1)} %get-tuple-element.258, ...), kind=kOutput, calls=%fused_computation.9.clone.1 | convolution fusion | flops 549453824 | bytes 18097664 | tf_op jit(solution)/shard_map/while/body/eval_jaxpr/qgd,kd->gqk/dot_general | solution.py:54
  242.0 3.3 bitcast_dynamic-update-slice_fusion.6
  246.4 2.6 fusion.46
  249.1 3.2 copy-done
  254.4 6.4 %fusion.47 = (f32[256,4]{0,1:T(4,128)S(1)}, bf16[128,4,256]{0,2,1:T(8,128)(2,1)S(1)}) fusion(bf16[1,256,4,128]{3,1,2,0:T(8,128)(2,1)S(1)} %copy.66, f32[2048,256,4]{1,0,2:T(8,128)} %copy-done, f32[4,256]{1,0:T(4,128)S(1)} %log_add_fusion.2, pred[256,2048]{0,1:T(8,128)(4,1)S(1)} %fusion.45, bf16[4,2048,128]{1,2,0:T(8,128)(2,1)} %get-tuple-element.257, ...), kind=kOutput, calls=%fused_computation.24.clone.1 | convolution fusion | flops 545782784 | bytes 9970176 | tf_op jit(solution)/shard_map/while/body/eval_jaxpr/gqk,kd->qgd/dot_general | solution.py:48
  260.8 5.6 %bitcast_dynamic-update-slice_fusion.7 = (bf16[4,4,256,2048]{2,3,1,0:T(8,128)(2,1)}, bf16[4,256,2048]{1,2,0:T(8,128)(2,1)S(1)}) fusion(bf16[4,4,256,2048]{2,3,1,0:T(8,128)(2,1)} %get-tuple-element.240, s32[]{:T(128)} %get-tuple-element.238, f32[4,256]{1,0:T(4,128)S(1)} %bitcast.168, bf16[4,256,4,128]{1,3,2,0:T(8,128)(2,1)S(1)} %get-tuple-element.258, ...), kind=kOutput, calls=%fused_computation.9.clone.1 | convolution fusion | flops 549453824 | bytes 18097664 | tf_op jit(solution)/shard_map/while/body/eval_jaxpr/qgd,kd->gqk/dot_general | solution.py:54
  268.2 3.2 bitcast_dynamic-update-slice_fusion.6
  272.2 13.4 %fusion.29 = f32[4,128,2048,1]{2,1,3,0:T(8,128)} fusion(bf16[4,4,256,2048]{2,3,1,0:T(8,128)(2,1)} %get-tuple-element.64, bf16[256,4,4,128]{0,3,2,1:T(8,128)(2,1)S(1)} %bitcast.162, pred[256]{0:T(512)(128)(4,1)S(1)} %broadcast_compare_fusion), kind=kOutput, calls=%fused_computation.46 | convolution fusion | flops 2148007936 | bytes 22020352 | tf_op jit(solution)/shard_map/cgqk,qcgd->kcd/dot_general | solution.py:89
  285.6 5.5 %copy.48 = f32[2048,512]{1,0:T(8,128)} copy(f32[2048,512]{0,1:T(8,128)} %bitcast.159) | data formatting | bytes 8388608 | tf_op jit(solution)/shard_map/reshape | solution.py:96
  291.0 11.4 %bitcast_multiply_fusion.1 = f32[4,2048,128]{1,2,0:T(8,128)} fusion(bf16[4,4,256,2048]{2,3,1,0:T(8,128)(2,1)} %get-tuple-element.63, bf16[256,4,4,128]{0,3,2,1:T(8,128)(2,1)S(1)} %bitcast.164), kind=kOutput, calls=%fused_computation.39 | convolution fusion | flops 2148532224 | bytes 22020096 | tf_op jit(solution)/shard_map/cgqk,qcgd->kcd/dot_general | solution.py:84
  302.4 5.3 %copy.47 = f32[2048,512]{1,0:T(8,128)} copy(f32[2048,512]{0,1:T(8,128)} %bitcast.160) | data formatting | bytes 8388608 | tf_op jit(solution)/shard_map/reshape | solution.py:95
  307.7 8.2 %pad_maximum_fusion = f32[2048,1024]{1,0:T(8,128)} fusion(f32[2048,512]{1,0:T(8,128)} %copy.48, f32[2048,512]{1,0:T(8,128)} %copy.47), kind=kLoop, calls=%fused_computation.38 | loop fusion | flops 2097152 | bytes 16777216 | tf_op jit(solution)/shard_map/concatenate | solution.py:93
  315.9 60.7 %psum.15 = f32[]{:T(128)} all-reduce(f32[]{:T(128)} %bitcast.22), channel_id=1, replica_groups=mesh['island'=32,'fsdp'=8] {'island'}, use_global_device_ids=true, to_apply=%region_7.8 | all-reduce | flops 1 | bytes 8 | tf_op jit(solution)/shard_map/psum | solution.py:108
  376.6 4.2 multiply_subtract_fusion
  386.8 112.1 %reduce-scatter.2.cloned.1.call-done = f32[256,1024]{1,0:T(8,128)} async-done(((f32[2048,1024]{1,0:T(8,128)}), f32[256,1024]{1,0:T(8,128)}) %reduce-scatter.2.cloned.1.call-update) | async-done | bytes 1048592 | tf_op jit(solution)/shard_map/reduce_scatter | solution.py:92
  (90 shorter events, 34.8 us)
Async XLA Ops:
  8.0 9.8 %copy-start.5 = (bf16[1,256,2048]{2,1,0:T(8,128)(2,1)S(1)}, bf16[1,256,2048]{2,1,0:T(8,128)(2,1)}, u32[]{:S(2)}) copy-start(bf16[1,256,2048]{2,1,0:T(8,128)(2,1)} %param.11) | copy-start | bytes 3145732
  8.0 83.4 %all-gather.3.cloned.1.call-start = ((), (), s32[]{:S(2)}) async-start(), calls=%async_computation.1 | async-start | bytes 2359296 | tf_op jit(solution)/shard_map/all_gather | solution.py:23
  9.9 157.2 %all-gather.5.cloned.1.call-start = ((), (), s32[]{:S(2)}) async-start(), calls=%async_computation.2 | async-start | bytes 2359296 | tf_op jit(solution)/shard_map/all_gather | solution.py:24
  11.8 364.8 %all-reduce.2.cloned.1.call-start = ((), (), s32[]{:S(2)}) async-start(), calls=%async_computation.4 | async-start | bytes 3145728 | tf_op jit(solution)/shard_map/psum | solution.py:108
  16.1 482.8 %reduce-scatter.2.cloned.1.call-start = ((), (), s32[]{:S(2)}) async-start(), calls=%async_computation.3 | async-start | bytes 9437184 | tf_op jit(solution)/shard_map/reduce_scatter | solution.py:92
  170.3 3.2 copy-start
  175.5 6.4 %copy-start.1 = (f32[2048,256,4]{1,0,2:T(8,128)S(1)}, f32[2048,256,4]{1,0,2:T(8,128)}, u32[]{:S(2)}) copy-start(f32[2048,256,4]{1,0,2:T(8,128)} %copy-done) | copy-start | bytes 25165828 | tf_op jit(solution)/shard_map/while
  182.0 5.7 %copy-start.6 = (bf16[4,256,4,128]{1,3,2,0:T(8,128)(2,1)S(1)}, bf16[4,256,4,128]{1,3,2,0:T(8,128)(2,1)}, u32[]{:S(2)}) copy-start(bf16[4,256,4,128]{1,3,2,0:T(8,128)(2,1)} %get-tuple-element.242) | copy-start | bytes 3145732 | tf_op jit(solution)/shard_map/while
  189.4 3.3 copy-start.7
  196.5 3.2 copy-start
  201.8 6.4 %copy-start.1 = (f32[2048,256,4]{1,0,2:T(8,128)S(1)}, f32[2048,256,4]{1,0,2:T(8,128)}, u32[]{:S(2)}) copy-start(f32[2048,256,4]{1,0,2:T(8,128)} %copy-done) | copy-start | bytes 25165828 | tf_op jit(solution)/shard_map/while
  208.2 5.7 %copy-start.6 = (bf16[4,256,4,128]{1,3,2,0:T(8,128)(2,1)S(1)}, bf16[4,256,4,128]{1,3,2,0:T(8,128)(2,1)}, u32[]{:S(2)}) copy-start(bf16[4,256,4,128]{1,3,2,0:T(8,128)(2,1)} %get-tuple-element.242) | copy-start | bytes 3145732 | tf_op jit(solution)/shard_map/while
  215.7 3.3 copy-start.7
  222.8 3.2 copy-start
  228.1 6.4 %copy-start.1 = (f32[2048,256,4]{1,0,2:T(8,128)S(1)}, f32[2048,256,4]{1,0,2:T(8,128)}, u32[]{:S(2)}) copy-start(f32[2048,256,4]{1,0,2:T(8,128)} %copy-done) | copy-start | bytes 25165828 | tf_op jit(solution)/shard_map/while
  234.5 5.7 %copy-start.6 = (bf16[4,256,4,128]{1,3,2,0:T(8,128)(2,1)S(1)}, bf16[4,256,4,128]{1,3,2,0:T(8,128)(2,1)}, u32[]{:S(2)}) copy-start(bf16[4,256,4,128]{1,3,2,0:T(8,128)(2,1)} %get-tuple-element.242) | copy-start | bytes 3145732 | tf_op jit(solution)/shard_map/while
  242.0 3.3 copy-start.7
  249.1 3.2 copy-start
  254.4 6.4 %copy-start.1 = (f32[2048,256,4]{1,0,2:T(8,128)S(1)}, f32[2048,256,4]{1,0,2:T(8,128)}, u32[]{:S(2)}) copy-start(f32[2048,256,4]{1,0,2:T(8,128)} %copy-done) | copy-start | bytes 25165828 | tf_op jit(solution)/shard_map/while
  260.8 5.7 %copy-start.6 = (bf16[4,256,4,128]{1,3,2,0:T(8,128)(2,1)S(1)}, bf16[4,256,4,128]{1,3,2,0:T(8,128)(2,1)}, u32[]{:S(2)}) copy-start(bf16[4,256,4,128]{1,3,2,0:T(8,128)(2,1)} %get-tuple-element.242) | copy-start | bytes 3145732 | tf_op jit(solution)/shard_map/while
  268.2 3.3 copy-start.7
  285.6 5.5 %copy-start.3 = (bf16[4,256,4,128]{1,3,2,0:T(8,128)(2,1)S(1)}, bf16[4,256,4,128]{1,3,2,0:T(8,128)(2,1)}, u32[]{:S(2)}) copy-start(bf16[4,256,4,128]{1,3,2,0:T(8,128)(2,1)} %get-tuple-element.270) | copy-start | bytes 3145732
  315.9 60.7 %copy-start.2 = (f32[96,4096]{1,0:T(8,128)S(1)}, f32[96,4096]{1,0:T(8,128)}, u32[]{:S(2)}) copy-start(f32[96,4096]{1,0:T(8,128)} %param.17) | copy-start | bytes 4718596
  315.9 60.7 %copy-start.4 = (f32[96,4096]{1,0:T(8,128)S(1)}, f32[96,4096]{1,0:T(8,128)}, u32[]{:S(2)}) copy-start(f32[96,4096]{1,0:T(8,128)} %param.19) | copy-start | bytes 4718596
Sparse Core Ops, SparseCore 0:
  11.9 79.4 all-gather.2
  94.4 72.6 all-gather.4
  316.1 182.8 reduce-scatter.1
Sparse Core Ops, SparseCore 1:
  16.2 314.6 all-reduce.1
where the time goes:
time: 509 us; the launch traced here: 508 us
  waiting for transfers between devices  260 us (51%)
  matrix products  90.7 us (18%)
  blocking collectives  60.7 us (12%)
  local copies, waits for them, and re-layouts  40.6 us (8%)
  other arithmetic  38.9 us (8%)
  between operations  16.6 us (3%)
    reduce_scatter x1, waiting for transfers between devices, body(): lax.psum_scatter(jnp.concatenate((key_part.reshape(lax.axis_size('fsdp')...  112 us
    all_gather x1, waiting for transfers between devices, body(): lax.all_gather(values, 'fsdp', axis=1, tiled=True)  75.8 us
    all_gather x1, waiting for transfers between devices, body(): lax.all_gather(keys, 'fsdp', axis=1, tiled=True)  72.2 us
    psum x1, blocking collectives, body(): weighted_sum, total_weight = lax.psum((drift_terms, weight), 'island')  60.7 us
    dot_general x4, matrix products, group_pass(): jnp.einsum('gqk,kd->qgd', soft_group, value_group, preferred_element_type...  25.6 us
    dot_general x4, matrix products, group_pass(): jnp.einsum('qgd,kd->gqk', masked_group, value_group, preferred_element_ty...  22.8 us
    dot_general x1, matrix products, body(): jnp.einsum('cgqk,qcgd->kcd', soft_rounded, head_masked, preferred_element...  13.4 us
    dynamic_update_slice x4, other arithmetic, body(): lax.map(group_pass, (jnp.transpose(query_head_rows, (1, 0, 2, 3)), jnp.tr...  13 us
  transfers between devices with their start and end apart: 4, of which 3 were waited for; matrix products, arithmetic and copies ran while one was open for 30% of the time, Pallas kernels for 0%

commit v1 on v0

v1 whole, which is shorter than its diff:
```python
import math
import jax
import jax.numpy as jnp
from jax import lax
from jax.experimental import pallas as pl
from jax.experimental.pallas import tpu as pltpu
from jax.sharding import PartitionSpec as P

HEAD = 128
GROUPS = 4
WIDE = 4
COLS = WIDE * HEAD
TILE = 256
neg_large = -1e30
score_scale = HEAD ** (-0.5)
exp2_scale = score_scale / math.log(2.0)
outer_momentum = 0.9
outer_rate = 0.7


def attend(place_ref, qg_ref, kv_ref, out_ref, dkv_ref,
           soft, q_rows, g_rows, q_cols, g_cols, k_cols, v_cols):
    step = pl.program_id(0)
    rows = qg_ref.shape[0]
    window = kv_ref.shape[0]
    tiles = window // TILE
    side, length = place_ref[0], place_ref[1]
    base = (2 * step + side) * rows
    full = jnp.minimum(base, length) // TILE
    live = jnp.minimum(base + rows, length + (TILE - 1)) // TILE

    @pl.when(step == 0)
    def _():
        dkv_ref[...] = jnp.zeros_like(dkv_ref)
        for j in range(tiles):
            span = slice(j * TILE, (j + 1) * TILE)
            k_cols[:, span] = kv_ref[span, :HEAD].astype(jnp.float32).T.astype(jnp.bfloat16)
            v_cols[:, span] = kv_ref[span, HEAD:].astype(jnp.float32).T.astype(jnp.bfloat16)

    row_id = base + lax.broadcasted_iota(jnp.int32, (rows, HEAD), 0)
    for h in range(WIDE):
        span = slice(h * rows, (h + 1) * rows)
        q_h = qg_ref[:, h * HEAD:(h + 1) * HEAD]
        g_h = qg_ref[:, COLS + h * HEAD:COLS + (h + 1) * HEAD]
        g_h = jnp.where(row_id < length, g_h.astype(jnp.float32), 0.0)
        q_rows[span, :] = q_h
        g_rows[span, :] = g_h.astype(jnp.bfloat16)
        q_cols[:, span] = q_h.astype(jnp.float32).T.astype(jnp.bfloat16)
        g_cols[:, span] = g_h.T.astype(jnp.bfloat16)

    def at(j):
        return pl.ds(pl.multiple_of(j * TILE, TILE), TILE)

    def held(j):
        return at(((j + side) % 2) * (tiles // 2) + j // 2)

    def score(j):
        return exp2_scale * jnp.dot(kv_ref[held(j), :HEAD], q_cols[...], preferred_element_type=jnp.float32)

    def score_full(j, top):
        s = score(j)
        soft[at(j), :] = s
        return jnp.maximum(top, jnp.max(s, axis=0, keepdims=True))

    def score_edge(j, top):
        s = score(j)
        key_pos = j * TILE + lax.broadcasted_iota(jnp.int32, (TILE, rows), 0)
        query_pos = base + lax.broadcasted_iota(jnp.int32, (TILE, rows), 1)
        keep = (key_pos <= query_pos) & (key_pos < length)
        s = jnp.where(jnp.concatenate([keep] * WIDE, axis=1), s, neg_large)
        soft[at(j), :] = s
        return jnp.maximum(top, jnp.max(s, axis=0, keepdims=True))

    top = jnp.full((1, WIDE * rows), neg_large, jnp.float32)
    top = lax.fori_loop(0, full, score_full, top)
    top = lax.fori_loop(full, live, score_edge, top)

    def weigh(j, total):
        e = jnp.exp2(soft[at(j), :] - top)
        soft[at(j), :] = e
        return total + jnp.sum(e, axis=0, keepdims=True)

    total = lax.fori_loop(0, live, weigh, jnp.zeros((1, WIDE * rows), jnp.float32))
    inverse = 1.0 / total

    def forward(j, context):
        p = soft[at(j), :] * inverse
        soft[at(j), :] = p
        p = p.astype(jnp.bfloat16)
        dkv_ref[held(j), HEAD:] += jnp.dot(p, g_rows[...], preferred_element_type=jnp.float32)
        return context + jnp.dot(v_cols[:, held(j)], p, preferred_element_type=jnp.float32)

    context = lax.fori_loop(0, live, forward, jnp.zeros((HEAD, WIDE * rows), jnp.float32))
    dots = jnp.sum(g_cols[...].astype(jnp.float32) * context, axis=0, keepdims=True)
    for h in range(WIDE):
        out_ref[:, h * HEAD:(h + 1) * HEAD] = context[:, h * rows:(h + 1) * rows].T.astype(jnp.bfloat16)

    def backward(j, q_grad):
        d = jnp.dot(kv_ref[held(j), HEAD:], g_cols[...], preferred_element_type=jnp.float32)
        d = (soft[at(j), :] * (d - dots)).astype(jnp.bfloat16)
        dkv_ref[held(j), :HEAD] += score_scale * jnp.dot(d, q_rows[...], preferred_element_type=jnp.float32)
        return q_grad + jnp.dot(k_cols[:, held(j)], d, preferred_element_type=jnp.float32)

    q_grad = lax.fori_loop(0, live, backward, jnp.zeros((HEAD, WIDE * rows), jnp.float32))
    for h in range(WIDE):
        lanes = slice(COLS + h * HEAD, COLS + (h + 1) * HEAD)
        out_ref[:, lanes] = (score_scale * q_grad[:, h * rows:(h + 1) * rows].T).astype(jnp.bfloat16)


def attention(place, qg, kv):
    blocks, rows, _ = qg.shape
    window = kv.shape[0]
    wide = WIDE * rows
    pairs = blocks * 2 * rows // TILE * blocks // 2 * WIDE
    return pl.pallas_call(
        attend,
        grid=(blocks,),
        in_specs=[
            pl.BlockSpec(memory_space=pltpu.SMEM),
            pl.BlockSpec((None, rows, 2 * COLS), lambda b: (b, 0, 0)),
            pl.BlockSpec((window, 2 * HEAD), lambda b: (0, 0)),
        ],
        out_specs=[
            pl.BlockSpec((None, rows, 2 * COLS), lambda b: (b, 0, 0)),
            pl.BlockSpec((window, 2 * HEAD), lambda b: (0, 0)),
        ],
        out_shape=[
            jax.ShapeDtypeStruct(qg.shape, jnp.bfloat16),
            jax.ShapeDtypeStruct((window, 2 * HEAD), jnp.float32),
        ],
        scratch_shapes=[
            pltpu.VMEM((window, wide), jnp.float32),
            pltpu.VMEM((wide, HEAD), jnp.bfloat16),
            pltpu.VMEM((wide, HEAD), jnp.bfloat16),
            pltpu.VMEM((HEAD, wide), jnp.bfloat16),
            pltpu.VMEM((HEAD, wide), jnp.bfloat16),
            pltpu.VMEM((HEAD, window), jnp.bfloat16),
            pltpu.VMEM((HEAD, window), jnp.bfloat16),
        ],
        compiler_params=pltpu.CompilerParams(vmem_limit_bytes=40 * 2**20),
        cost_estimate=pl.CostEstimate(
            flops=pairs * 10 * TILE * TILE * HEAD, bytes_accessed=8 * 2**20, transcendentals=pairs * TILE * TILE),
    )(place, qg, kv)


def body(queries, keys, values, d_out, lengths, steps, theta_global, theta_local, momentum):
    rows = queries.shape[1]
    key_width = keys.shape[2]
    ranks = lax.axis_size("fsdp")
    islands = lax.axis_size("island")
    across = [[2 * i + side for i in range(ranks // 2)] for side in range(2)]
    other = [(i, i ^ 1) for i in range(ranks)]
    side = lax.axis_index("fsdp") % 2
    place = jnp.stack([side.astype(jnp.int32), lengths[0]])

    def spread(x):
        return lax.all_to_all(x, "fsdp", 0, 0, axis_index_groups=across, tiled=True)

    def by_group(x):
        return jnp.transpose(x.reshape(rows, GROUPS, -1), (1, 0, 2))

    def by_row(x, width):
        return jnp.transpose(x, (1, 0, 2)).reshape(1, rows, width)

    kv = spread(jnp.concatenate([by_group(keys[0]), by_group(values[0])], axis=2))
    kv_other = lax.ppermute(kv, "fsdp", other)
    qg = spread(jnp.concatenate([by_group(queries[0]), by_group(d_out[0])], axis=2))
    window = 2 * GROUPS * rows
    out, part = attention(place, qg, jnp.concatenate([kv, kv_other], axis=0).reshape(window, 2 * HEAD))
    part = part.reshape(2, GROUPS, rows, 2 * HEAD)
    out = spread(out)
    context = by_row(out[:, :, :COLS], queries.shape[2])
    d_queries = by_row(out[:, :, COLS:], queries.shape[2])
    total = part[0] + lax.ppermute(part[1], "fsdp", other)
    grads = spread(total.astype(jnp.bfloat16))
    d_keys = by_row(grads[:, :, :HEAD], key_width)
    d_values = by_row(grads[:, :, HEAD:], key_width)

    frag_rows, width = theta_global.shape
    piece = width // islands
    note = jnp.stack([steps[0], lengths[0] // 16, lengths[0] % 16]).astype(jnp.bfloat16)
    note = jnp.broadcast_to(jnp.pad(note, (0, piece - 3)), (islands, 16, piece))
    local = jnp.transpose(theta_local[0].reshape(frag_rows, islands, piece), (1, 0, 2))
    local = lax.all_to_all(jnp.concatenate([local, note], axis=1), "island", 0, 0, tiled=True).astype(jnp.float32)
    note = local[:, frag_rows, :]
    weight = note[:, 0] * (16.0 * note[:, 1] + note[:, 2])
    mine = lax.dynamic_slice(theta_global, (0, lax.axis_index("island") * piece), (frag_rows, piece))
    pseudo = jnp.sum(weight[:, None, None] * (mine[None] - local[:, :frag_rows]), axis=0) / jnp.sum(weight)
    pseudo = lax.all_gather(pseudo, "island", axis=0)
    pseudo = jnp.transpose(pseudo, (1, 0, 2)).reshape(frag_rows, width)
    momentum_new = outer_momentum * momentum + pseudo
    theta_new = theta_global - outer_rate * (pseudo + outer_momentum * momentum_new)
    return (context, d_queries, d_keys, d_values, theta_new, momentum_new)


def solution(mesh):
    seq = P("island", "fsdp", None)
    return jax.shard_map(
        body,
        mesh=mesh,
        in_specs=(seq, seq, seq, seq, P("island"), P("island"), P("fsdp", None), seq, P("fsdp", None)),
        out_specs=(seq, seq, seq, seq, P("fsdp", None), P("fsdp", None)),
        check_vma=False,
    )
```

time: 509 us -> 236 us (0.46)
  waiting for transfers between devices: 260 us -> 136 us
  matrix products: 90.7 us -> 0 us
  blocking collectives: 60.7 us -> 12.4 us
  starting transfers between devices: 0.16 us -> 28 us
  other arithmetic: 38.9 us -> 11.2 us
  local copies, waits for them, and re-layouts: 40.6 us -> 15.8 us
  Pallas kernels: 0 us -> 15.3 us
    all_gather x2 -> x1, waiting for transfers between devices: 148 us -> 0.01 us  [body(): pseudo = lax.all_gather(pseudo, 'island', axis=0)]
    reduce_scatter x1 -> x0, waiting for transfers between devices: 112 us -> none  [body(): lax.psum_scatter(jnp.concatenate((key_part.reshape(lax.axis_size('fsdp')...]
    dot_general x18 -> x0, matrix products: 90.7 us -> none  [the longest x4 25.6 us: group_pass(): jnp.einsum('gqk,kd->qgd', soft_group, value_group, preferred_element_type...]
    ppermute x0 -> x2, waiting for transfers between devices: none -> 84.3 us  [the longest x1 46.2 us: body(): total = part[0] + lax.ppermute(part[1], 'fsdp', other)]
    psum x1 -> x0, blocking collectives: 60.7 us -> none  [body(): weighted_sum, total_weight = lax.psum((drift_terms, weight), 'island')]
    all_to_all x0 -> x4, waiting for transfers between devices: none -> 51.4 us  [the longest x3 51.4 us: spread(): return lax.all_to_all(x, 'fsdp', 0, 0, axis_index_groups=across, tiled=True)]
    all_to_all x0 -> x4, starting transfers between devices: none -> 20.5 us  [the longest x3 11.5 us: spread(): return lax.all_to_all(x, 'fsdp', 0, 0, axis_index_groups=across, tiled=True)]
    pallas_call x0 -> x1, Pallas kernels: none -> 15.3 us  [attention(): pl.pallas_call(attend, grid=(blocks,), in_specs=[pl.BlockSpec(memory_spac...]
  transfers between devices with their start and end apart: 4 -> 7, of which waited for: 3 -> 5; matrix products, arithmetic and copies ran while one was open for 30% -> 9% of each run, Pallas kernels for 0% -> 7%
where the time goes in v1:
time: 236 us; the launch traced here: 234 us
  waiting for transfers between devices  136 us (58%)
  starting transfers between devices  28 us (12%)
  local copies, waits for them, and re-layouts  15.8 us (7%)
  between operations  15.6 us (7%)
  Pallas kernels  15.3 us (6%)
  blocking collectives  12.4 us (5%)
  other arithmetic  11.2 us (5%)
    all_to_all x3, waiting for transfers between devices, spread(): return lax.all_to_all(x, 'fsdp', 0, 0, axis_index_groups=across, tiled=True)  51.4 us
    ppermute x1, waiting for transfers between devices, body(): total = part[0] + lax.ppermute(part[1], 'fsdp', other)  46.2 us
    ppermute x1, waiting for transfers between devices, body(): kv_other = lax.ppermute(kv, 'fsdp', other)  38.1 us
    pallas_call x1, Pallas kernels, attention(): pl.pallas_call(attend, grid=(blocks,), in_specs=[pl.BlockSpec(memory_spac...  15.3 us
    all_to_all x1, blocking collectives, spread(): return lax.all_to_all(x, 'fsdp', 0, 0, axis_index_groups=across, tiled=True)  12.4 us
    all_to_all x3, starting transfers between devices, spread(): return lax.all_to_all(x, 'fsdp', 0, 0, axis_index_groups=across, tiled=True)  11.5 us
    all_to_all x1, starting transfers between devices, body(): lax.all_to_all(jnp.concatenate([local, note], axis=1), 'island', 0, 0, ti...  9.02 us
    unnamed x11, local copies, waits for them, and re-layouts  5.08 us
  transfers between devices with their start and end apart: 7, of which 5 were waited for; matrix products, arithmetic and copies ran while one was open for 9% of the time, Pallas kernels for 7%

profile of v1, /device:TPU:16, one launch (start us, length us, event | category | flops | bytes accessed | tf_op | source)
XLA Modules:
  0.0 234.0 jit_solution(10881804010038390339)
XLA Ops:
  7.2 1.0 reshape_squeeze.18
  8.2 1.0 reshape_squeeze.17
  9.3 0.9 pad_maximum_fusion.3
  10.2 4.3 %all-to-all-start.1 = ((bf16[4,256,256]{2,1,0:T(8,128)(2,1)}), bf16[4,256,256]{2,1,0:T(8,128)(2,1)}, u32[]{:S(2)}, u32[]{:S(2)}) async-start(bf16[4,256,256]{2,1,0:T(8,128)(2,1)} %pad_maximum_fusion.3), calls=%async_computation.1 | async-start | bytes 1048576 | tf_op jit(solution)/shard_map/all_to_all | solution.py:157
  15.0 0.5 copy.63
  15.5 1.5 copy.60
  17.6 1.7 pad_maximum_fusion
  19.2 4.9 %all-to-all-done.1 = bf16[4,256,256]{2,1,0:T(8,128)(2,1)} async-done(((bf16[4,256,256]{2,1,0:T(8,128)(2,1)}), bf16[4,256,256]{2,1,0:T(8,128)(2,1)}, u32[]{:S(2)}, u32[]{:S(2)}) %all-to-all-start.1) | async-done | bytes 524320 | tf_op jit(solution)/shard_map/all_to_all | solution.py:157
  24.1 3.6 %all-to-all-start = ((bf16[4,256,1024]{2,1,0:T(8,128)(2,1)}), bf16[4,256,1024]{2,1,0:T(8,128)(2,1)S(1)}, u32[]{:S(2)}, u32[]{:S(2)}) async-start(bf16[4,256,1024]{2,1,0:T(8,128)(2,1)} %pad_maximum_fusion), calls=%async_computation | async-start | bytes 4194304 | tf_op jit(solution)/shard_map/all_to_all | solution.py:157
  29.7 1.0 pad_maximum_fusion.2
  30.6 22.6 %all-to-all-done.qg_ref = bf16[4,256,1024]{2,1,0:T(8,128)(2,1)S(1)} async-done(((bf16[4,256,1024]{2,1,0:T(8,128)(2,1)}), bf16[4,256,1024]{2,1,0:T(8,128)(2,1)S(1)}, u32[]{:S(2)}, u32[]{:S(2)}) %all-to-all-start) | async-done | bytes 2097184 | tf_op jit(solution)/shard_map/all_to_all | solution.py:157
  53.2 9.0 %all-to-all-start.4 = ((bf16[32,112,128]{2,1,0:T(8,128)(2,1)}), bf16[32,112,128]{2,1,0:T(8,128)(2,1)S(1)}, u32[]{:S(2)}, u32[]{:S(2)}) async-start(bf16[32,112,128]{2,1,0:T(8,128)(2,1)} %pad_maximum_fusion.2), calls=%async_computation.4 | async-start | bytes 1835008 | tf_op jit(solution)/shard_map/all_to_all | solution.py:184
  62.3 4.6 %collective-permute-start = (bf16[4,256,256]{2,1,0:T(8,128)(2,1)}, bf16[4,256,256]{2,1,0:T(8,128)(2,1)S(1)}, u32[]{:S(2)}, u32[]{:S(2)}) collective-permute-start(bf16[4,256,256]{2,1,0:T(8,128)(2,1)} %all-to-all-done.1), channel_id=1, source_target_pairs={{0,1},{1,0},{2,3},{3,2},{4,5},{5,4},{6,7},{7,6},{8,9},{9,8},{10,11... | collective-permute-start | bytes 1572872 | tf_op jit(solution)/shard_map/ppermute | solution.py:166
  66.9 38.1 %collective-permute-done = bf16[4,256,256]{2,1,0:T(8,128)(2,1)S(1)} collective-permute-done((bf16[4,256,256]{2,1,0:T(8,128)(2,1)}, bf16[4,256,256]{2,1,0:T(8,128)(2,1)S(1)}, u32[]{:S(2)}, u32[]{:S(2)}) %collective-permute-start) | collective-permute-done | bytes 524320 | tf_op jit(solution)/shard_map/ppermute | solution.py:166
  105.0 1.1 pad_maximum_fusion.1
  106.2 15.3 %shard_map.136 = (bf16[4,256,1024]{2,1,0:T(8,128)(2,1)}, f32[2048,256]{1,0:T(8,128)S(1)}) custom-call(s32[2]{0:T(128)S(1)} %pad_add_fusion.place_ref, bf16[4,256,1024]{2,1,0:T(8,128)(2,1)S(1)} %all-to-all-done.qg_ref, bf16[2048,256]{1,0:T(8,128)(2,1)S(1)} %bitcast.47), custom_call_target="tpu_custom_call" | custom-call | flops 5368709120 | bytes 8388608 | tf_op jit(solution)/shard_map/pallas_call | solution.py:115
  121.5 1.1 fusion.7
  122.6 2.9 %collective-permute-start.1 = (f32[4,256,256]{2,1,0:T(8,128)}, f32[4,256,256]{2,1,0:T(8,128)S(1)}, u32[]{:S(2)}, u32[]{:S(2)}) collective-permute-start(f32[4,256,256]{2,1,0:T(8,128)} %bitcast.13), channel_id=1, source_target_pairs={{0,1},{1,0},{2,3},{3,2},{4,5},{5,4},{6,7},{7,6},{8,9},{9,8},{10,11... | collective-permute-start | bytes 3145736 | tf_op jit(solution)/shard_map/ppermute | solution.py:174
  125.5 0.8 constant_dynamic-slice_fusion
  126.4 0.7 fusion.5
  127.3 1.3 broadcast_divide_fusion
  128.6 46.2 %collective-permute-done.1 = f32[4,256,256]{2,1,0:T(8,128)S(1)} collective-permute-done((f32[4,256,256]{2,1,0:T(8,128)}, f32[4,256,256]{2,1,0:T(8,128)S(1)}, u32[]{:S(2)}, u32[]{:S(2)}) %collective-permute-start.1) | collective-permute-done | bytes 1048608 | tf_op jit(solution)/shard_map/ppermute | solution.py:174
  175.0 12.4 %all_to_all.25 = bf16[4,256,256]{2,1,0:T(8,128)(2,1)S(1)} all-to-all(bf16[4,256,256]{2,1,0:T(8,128)(2,1)S(1)} %add_convert_fusion), channel_id=1, replica_groups={{0,2,4,6},{1,3,5,7},{8,10,12,14},{9,11,13,15},{16,18,20,22},{17,19,21,2..., dimensions={0} | all-to-all | bytes 1048576 | tf_op jit(solution)/shard_map/all_to_all | solution.py:157
  187.4 3.6 %all-to-all-start.2 = ((bf16[4,256,1024]{2,1,0:T(8,128)(2,1)}), bf16[4,256,1024]{2,1,0:T(8,128)(2,1)S(1)}, u32[]{:S(2)}, u32[]{:S(2)}) async-start(bf16[4,256,1024]{2,1,0:T(8,128)(2,1)} %get-tuple-element.8), calls=%async_computation.2 | async-start | bytes 4194304 | tf_op jit(solution)/shard_map/all_to_all | solution.py:157
  191.4 0.8 reshape.67
  192.4 0.8 reshape.68
  193.2 23.9 %all-to-all-done.2 = bf16[4,256,1024]{2,1,0:T(8,128)(2,1)S(1)} async-done(((bf16[4,256,1024]{2,1,0:T(8,128)(2,1)}), bf16[4,256,1024]{2,1,0:T(8,128)(2,1)S(1)}, u32[]{:S(2)}, u32[]{:S(2)}) %all-to-all-start.2) | async-done | bytes 2097184 | tf_op jit(solution)/shard_map/all_to_all | solution.py:157
  217.1 1.2 slice_bitcast_fusion
  218.3 1.5 copy.66
  219.7 1.4 copy.72
  221.7 1.4 copy.73
  223.2 3.9 %fusion.1 = (f32[96,4096]{1,0:T(8,128)}, f32[96,4096]{1,0:T(8,128)}) fusion(f32[96,4096]{1,0:T(8,128)S(1)} %copy-done, f32[32,12,8,128]{3,2,1,0:T(8,128)} %bitcast.56, f32[96,4096]{1,0:T(8,128)} %param.17), kind=kLoop, calls=%fused_computation.4 | loop fusion | flops 2359296 | bytes 7864320 | tf_op jit(solution)/shard_map/sub | solution.py:192
  (26 shorter events, 3.5 us)
Async XLA Ops:
  9.2 5.2 %copy-start.1 = (bf16[1,256,2048]{2,1,0:T(8,128)(2,1)S(1)}, bf16[1,256,2048]{2,1,0:T(8,128)(2,1)}, u32[]{:S(2)}) copy-start(bf16[1,256,2048]{2,1,0:T(8,128)(2,1)} %param.12) | copy-start | bytes 3145732
  10.2 14.0 %all-to-all-start.1 = ((bf16[4,256,256]{2,1,0:T(8,128)(2,1)}), bf16[4,256,256]{2,1,0:T(8,128)(2,1)}, u32[]{:S(2)}, u32[]{:S(2)}) async-start(bf16[4,256,256]{2,1,0:T(8,128)(2,1)} %pad_maximum_fusion.3), calls=%async_computation.1 | async-start | bytes 1048576 | tf_op jit(solution)/shard_map/all_to_all | solution.py:157
  19.2 9.9 %copy-start.2 = (bf16[1,96,4096]{2,1,0:T(8,128)(2,1)S(1)}, bf16[1,96,4096]{2,1,0:T(8,128)(2,1)}, u32[]{:S(2)}) copy-start(bf16[1,96,4096]{2,1,0:T(8,128)(2,1)} %param.16) | copy-start | bytes 2359300
  24.1 29.1 %all-to-all-start = ((bf16[4,256,1024]{2,1,0:T(8,128)(2,1)}), bf16[4,256,1024]{2,1,0:T(8,128)(2,1)S(1)}, u32[]{:S(2)}, u32[]{:S(2)}) async-start(bf16[4,256,1024]{2,1,0:T(8,128)(2,1)} %pad_maximum_fusion), calls=%async_computation | async-start | bytes 4194304 | tf_op jit(solution)/shard_map/all_to_all | solution.py:157
  53.2 73.1 %all-to-all-start.4 = ((bf16[32,112,128]{2,1,0:T(8,128)(2,1)}), bf16[32,112,128]{2,1,0:T(8,128)(2,1)S(1)}, u32[]{:S(2)}, u32[]{:S(2)}) async-start(bf16[32,112,128]{2,1,0:T(8,128)(2,1)} %pad_maximum_fusion.2), calls=%async_computation.4 | async-start | bytes 1835008 | tf_op jit(solution)/shard_map/all_to_all | solution.py:184
  62.2 160.9 %all-gather.3.cloned.1.call-start = ((), (), s32[]{:S(2)}) async-start(), calls=%async_computation.5 | async-start | bytes 1622016 | tf_op jit(solution)/shard_map/all_gather | solution.py:189
  62.3 42.8 %collective-permute-start = (bf16[4,256,256]{2,1,0:T(8,128)(2,1)}, bf16[4,256,256]{2,1,0:T(8,128)(2,1)S(1)}, u32[]{:S(2)}, u32[]{:S(2)}) collective-permute-start(bf16[4,256,256]{2,1,0:T(8,128)(2,1)} %all-to-all-done.1), channel_id=1, source_target_pairs={{0,1},{1,0},{2,3},{3,2},{4,5},{5,4},{6,7},{7,6},{8,9},{9,8},{10,11... | collective-permute-start | bytes 1572872 | tf_op jit(solution)/shard_map/ppermute | solution.py:166
  122.6 52.2 %collective-permute-start.1 = (f32[4,256,256]{2,1,0:T(8,128)}, f32[4,256,256]{2,1,0:T(8,128)S(1)}, u32[]{:S(2)}, u32[]{:S(2)}) collective-permute-start(f32[4,256,256]{2,1,0:T(8,128)} %bitcast.13), channel_id=1, source_target_pairs={{0,1},{1,0},{2,3},{3,2},{4,5},{5,4},{6,7},{7,6},{8,9},{9,8},{10,11... | collective-permute-start | bytes 3145736 | tf_op jit(solution)/shard_map/ppermute | solution.py:174
  187.4 29.6 %all-to-all-start.2 = ((bf16[4,256,1024]{2,1,0:T(8,128)(2,1)}), bf16[4,256,1024]{2,1,0:T(8,128)(2,1)S(1)}, u32[]{:S(2)}, u32[]{:S(2)}) async-start(bf16[4,256,1024]{2,1,0:T(8,128)(2,1)} %get-tuple-element.8), calls=%async_computation.2 | async-start | bytes 4194304 | tf_op jit(solution)/shard_map/all_to_all | solution.py:157
  221.7 1.5 copy-start
Sparse Core Ops, SparseCore 0:
  128.7 81.7 all-gather.2

commit v2 on v0

v2 whole, which is shorter than its diff:
```python
import math
import jax
import jax.numpy as jnp
from jax import lax
from jax.experimental import pallas as pl
from jax.experimental.pallas import tpu as pltpu
from jax.sharding import PartitionSpec as P

HEAD = 128
GROUPS = 4
WIDE = 4
COLS = WIDE * HEAD
TILE = 512
NOTE = 16
neg_large = -1e30
score_scale = HEAD ** (-0.5)
exp2_scale = score_scale / math.log(2.0)
outer_momentum = 0.9
outer_rate = 0.7
f32 = jnp.float32
bf16 = jnp.bfloat16


def call(kernel, place, ins, outs, scratch=(), flops=0, exps=0, vmem=58):
    def whole(a):
        zeros = (0,) * len(a.shape)
        return pl.BlockSpec(a.shape, lambda: zeros)

    outs = [jax.ShapeDtypeStruct(s, t) for s, t in outs]
    size = sum(math.prod(a.shape) * a.dtype.itemsize for a in [*ins, *outs])
    return pl.pallas_call(
        kernel,
        in_specs=[pl.BlockSpec(memory_space=pltpu.SMEM)] + [whole(a) for a in ins],
        out_specs=[whole(a) for a in outs],
        out_shape=outs,
        scratch_shapes=[pltpu.VMEM(s, t) for s, t in scratch],
        compiler_params=pltpu.CompilerParams(vmem_limit_bytes=vmem * 2**20),
        cost_estimate=pl.CostEstimate(flops=flops, bytes_accessed=size if flops else 0, transcendentals=exps),
    )(place, *ins)


def after(earlier, later):
    return lax.optimization_barrier((earlier, later))[1]


def at(j):
    return pl.ds(pl.multiple_of(j * TILE, TILE), TILE)


def turn(x):
    return x.astype(f32).T.astype(bf16)


def source(place_ref, r):
    return (place_ref[0] + GROUPS - r) % GROUPS


def key_rows(place_ref, r, other):
    side = place_ref[1]
    block = 2 * source(place_ref, r) + ((1 - side) if other else side)
    return pl.ds(pl.multiple_of(block * (TILE // 2), TILE // 2), TILE // 2)


def lanes(index, width):
    return pl.ds(pl.multiple_of(index * width, width), width)


def extent(place_ref, r, rows):
    side, length = place_ref[1], place_ref[2]
    base = (2 * source(place_ref, r) + side) * rows
    live = (jnp.minimum(base + rows, length) + (TILE - 1)) // TILE
    return base, length, live


def keep_mask(j, base, length, rows):
    key_pos = j * TILE + lax.broadcasted_iota(jnp.int32, (TILE, rows), 0)
    query_pos = base + lax.broadcasted_iota(jnp.int32, (TILE, rows), 1)
    keep = (key_pos <= query_pos) & (key_pos < length)
    return jnp.concatenate([keep] * WIDE, axis=1)


def forward_kernel(place_ref, *refs):
    qg_refs, (near_ref, far_ref), refs = refs[:GROUPS], refs[GROUPS:GROUPS + 2], refs[GROUPS + 2:]
    ctx_refs, (near_out, far_out, stat_ref), refs = refs[:GROUPS], refs[GROUPS:GROUPS + 3], refs[GROUPS + 3:]
    soft, q_cols, g_cols, g_rows, v_cols, kv_ref, dv_ref = refs
    rows = qg_refs[0].shape[0]
    window = kv_ref.shape[0]
    wide = WIDE * rows
    dv_ref[...] = jnp.zeros_like(dv_ref)
    for r in range(GROUPS):
        kv_ref[key_rows(place_ref, r, False), :] = near_ref[r]
        kv_ref[key_rows(place_ref, r, True), :] = far_ref[r]
    for j in range(window // rows):
        span = slice(j * rows, (j + 1) * rows)
        v_cols[:, span] = turn(kv_ref[span, HEAD:])
    for r in range(GROUPS):
        base, length, live = extent(place_ref, r, rows)
        qg_ref = qg_refs[r]
        row_id = base + lax.broadcasted_iota(jnp.int32, (rows, HEAD), 0)
        for h in range(WIDE):
            span = slice(h * rows, (h + 1) * rows)
            g_h = qg_ref[:, COLS + h * HEAD:COLS + (h + 1) * HEAD]
            g_h = jnp.where(row_id < length, g_h.astype(f32), 0.0)
            g_rows[span, :] = g_h.astype(bf16)
            q_cols[:, span] = turn(qg_ref[:, h * HEAD:(h + 1) * HEAD])
            g_cols[:, span] = g_h.T.astype(bf16)

        def score(j):
            return exp2_scale * jnp.dot(kv_ref[at(j), :HEAD], q_cols[...], preferred_element_type=f32)

        def score_full(j, top):
            s = score(j)
            soft[at(j), :] = s
            return jnp.maximum(top, jnp.max(s, axis=0, keepdims=True))

        top = lax.fori_loop(0, live - 1, score_full, jnp.full((1, wide), neg_large, f32))
        s = jnp.where(keep_mask(live - 1, base, length, rows), score(live - 1), neg_large)
        soft[at(live - 1), :] = s
        top = jnp.maximum(top, jnp.max(s, axis=0, keepdims=True))

        def weigh(j, total):
            e = jnp.exp2(soft[at(j), :] - top)
            soft[at(j), :] = e
            return total + jnp.sum(e, axis=0, keepdims=True)

        total = lax.fori_loop(0, live, weigh, jnp.zeros((1, wide), f32))
        inverse = 1.0 / total

        def forward(j, context):
            p = (soft[at(j), :] * inverse).astype(bf16)
            dv_ref[at(j), :] += jnp.dot(p, g_rows[...], preferred_element_type=f32)
            return context + jnp.dot(v_cols[:, at(j)], p, preferred_element_type=f32)

        context = lax.fori_loop(0, live, forward, jnp.zeros((HEAD, wide), f32))
        stat_ref[r, 0:1, :] = top
        stat_ref[r, 1:2, :] = inverse
        stat_ref[r, 2:3, :] = jnp.sum(g_cols[...].astype(f32) * context, axis=0, keepdims=True)
        for h in range(WIDE):
            ctx_refs[r][:, h * HEAD:(h + 1) * HEAD] = context[:, h * rows:(h + 1) * rows].T.astype(bf16)
    for r in range(GROUPS):
        near_out[r] = dv_ref[key_rows(place_ref, r, False), :]
        far_out[r] = dv_ref[key_rows(place_ref, r, True), :].astype(bf16)


def backward_kernel(place_ref, *refs):
    qg_refs, (near_ref, far_ref, stat_ref), refs = refs[:GROUPS], refs[GROUPS:GROUPS + 3], refs[GROUPS + 3:]
    dq_refs, (near_out, far_out), refs = refs[:GROUPS], refs[GROUPS:GROUPS + 2], refs[GROUPS + 2:]
    q_cols, g_cols, q_rows, k_cols, dq_cols, kv_ref, dk_ref = refs
    rows = qg_refs[0].shape[0]
    window = kv_ref.shape[0]
    dk_ref[...] = jnp.zeros_like(dk_ref)
    for r in range(GROUPS):
        kv_ref[key_rows(place_ref, r, False), :] = near_ref[r]
        kv_ref[key_rows(place_ref, r, True), :] = far_ref[r]
    for j in range(window // rows):
        span = slice(j * rows, (j + 1) * rows)
        k_cols[:, span] = turn(kv_ref[span, :HEAD])
    for r in range(GROUPS):
        base, length, live = extent(place_ref, r, rows)
        qg_ref = qg_refs[r]
        row_id = base + lax.broadcasted_iota(jnp.int32, (rows, HEAD), 0)
        for h in range(WIDE):
            span = slice(h * rows, (h + 1) * rows)
            q_h = qg_ref[:, h * HEAD:(h + 1) * HEAD]
            g_h = qg_ref[:, COLS + h * HEAD:COLS + (h + 1) * HEAD]
            g_h = jnp.where(row_id < length, g_h.astype(f32), 0.0)
            q_rows[span, :] = q_h
            q_cols[:, span] = turn(q_h)
            g_cols[:, span] = g_h.T.astype(bf16)

        def backward(j, edge):
            s = exp2_scale * jnp.dot(kv_ref[at(j), :HEAD], q_cols[...], preferred_element_type=f32)
            if edge:
                s = jnp.where(keep_mask(j, base, length, rows), s, neg_large)
            p = jnp.exp2(s - stat_ref[r, 0:1, :]) * stat_ref[r, 1:2, :]
            d = jnp.dot(kv_ref[at(j), HEAD:], g_cols[...], preferred_element_type=f32)
            d = (p * (d - stat_ref[r, 2:3, :])).astype(bf16)
            dk_ref[at(j), :] += score_scale * jnp.dot(d, q_rows[...], preferred_element_type=f32)
            return jnp.dot(k_cols[:, at(j)], d, preferred_element_type=f32)

        dq_cols[...] = backward(live - 1, True)

        def step(j, carry):
            dq_cols[...] += backward(j, False)
            return carry

        lax.fori_loop(0, live - 1, step, 0)
        for h in range(WIDE):
            dq_refs[r][:, h * HEAD:(h + 1) * HEAD] = (score_scale * dq_cols[:, h * rows:(h + 1) * rows].T).astype(bf16)
    for r in range(GROUPS):
        near_out[r] = dk_ref[key_rows(place_ref, r, False), :]
        far_out[r] = dk_ref[key_rows(place_ref, r, True), :].astype(bf16)


def forward_call(place, blocks, near, far):
    groups, rows, _ = near.shape
    window, wide = 2 * groups * rows, WIDE * rows
    near_part, far_part = ((groups, rows, HEAD), f32), ((groups, rows, HEAD), bf16)
    return call(
        forward_kernel, place, [*blocks, near, far],
        [((rows, COLS), bf16)] * groups + [near_part, far_part, ((groups, 8, wide), f32)],
        [((window, wide), f32), ((HEAD, wide), bf16), ((HEAD, wide), bf16), ((wide, HEAD), bf16), ((HEAD, window), bf16),
         ((window, 2 * HEAD), bf16), ((window, HEAD), f32)],
        flops=12 * 10**9, exps=10**7, vmem=58)


def backward_call(place, blocks, near, far, stat):
    groups, rows, _ = near.shape
    window, wide = 2 * groups * rows, WIDE * rows
    near_part, far_part = ((groups, rows, HEAD), f32), ((groups, rows, HEAD), bf16)
    return call(
        backward_kernel, place, [*blocks, near, far, stat],
        [((rows, COLS), bf16)] * groups + [near_part, far_part],
        [((HEAD, wide), bf16), ((HEAD, wide), bf16), ((wide, HEAD), bf16), ((HEAD, window), bf16), ((HEAD, wide), f32),
         ((window, 2 * HEAD), bf16), ((window, HEAD), f32)],
        flops=12 * 10**9, exps=10**7, vmem=58)


def pack_kernel(place_ref, k_ref, v_ref, q_ref, g_ref, local_ref, note_ref, *refs):
    pair_refs, block_refs, sent_ref = refs[:GROUPS], refs[GROUPS:2 * GROUPS], refs[2 * GROUPS]
    for out_refs, ins, width in ((pair_refs, (k_ref, v_ref), HEAD), (block_refs, (q_ref, g_ref), COLS)):
        for r in range(GROUPS):
            for i, ref in enumerate(ins):
                out_refs[r][:, i * width:(i + 1) * width] = ref[:, lanes((place_ref[0] + r) % GROUPS, width)]
    width = sent_ref.shape[2]
    for i in range(sent_ref.shape[0]):
        sent_ref[i, :-NOTE, :] = local_ref[:, i * width:(i + 1) * width]
        sent_ref[i, -NOTE:, :] = note_ref[...]


def pack(place, k, v, q, g, local, note):
    rows, (note_rows, line) = k.shape[0], note.shape
    return call(
        pack_kernel, place, [k, v, q, g, local, note],
        [((rows, 2 * HEAD), bf16)] * GROUPS + [((rows, 2 * COLS), bf16)] * GROUPS
        + [((local.shape[1] // line, local.shape[0] + note_rows, line), bf16)])


def unpack_kernel(place_ref, *refs):
    ins, outs = refs[:GROUPS], refs[GROUPS:]
    width = outs[0].shape[1] // GROUPS
    for r in range(GROUPS):
        for i, out in enumerate(outs):
            out[:, lanes((place_ref[0] + r) % GROUPS, width)] = ins[r][:, i * width:(i + 1) * width]


def unpack(place, blocks, count):
    rows, width = blocks[0].shape
    return call(unpack_kernel, place, blocks, [((rows, GROUPS * width // count), bf16)] * count)


def merge_kernel(place_ref, dk_near, dk_far, dv_near, dv_far, *out_refs):
    for r in range(GROUPS):
        out_refs[r][:, :HEAD] = (dk_near[r] + dk_far[r].astype(f32)).astype(bf16)
        out_refs[r][:, HEAD:] = (dv_near[r] + dv_far[r].astype(f32)).astype(bf16)


def theta_sum_kernel(place_ref, g_ref, in_ref, out_ref):
    frag_rows, (count, _, width) = g_ref.shape[0], out_ref.shape
    for part in range(count):
        span = slice(part * width, (part + 1) * width)
        g = g_ref[:, lanes(place_ref[3] * count + part, width)]
        total, drift = 0.0, 0.0
        for i in range(in_ref.shape[0]):
            note = in_ref[i, frag_rows:, span].astype(f32)
            weight = note[0:1, :] * (16.0 * note[1:2, :] + note[2:3, :])
            total = total + weight
            drift = drift + weight * (g - in_ref[i, :frag_rows, span].astype(f32))
        out_ref[part, :frag_rows, :] = drift
        out_ref[part, frag_rows:, :] = jnp.broadcast_to(total, (8, width))


def theta_mean_kernel(place_ref, in_ref, out_ref):
    total = (in_ref[0] + in_ref[1]) + (in_ref[2] + in_ref[3])
    mean = total[:-8] / total[-8:-7]
    for part in range(out_ref.shape[0]):
        out_ref[part] = mean


def theta_update_kernel(place_ref, near_ref, far_ref, g_ref, m_ref, theta_ref, moment_ref):
    count, _, width = near_ref.shape
    for c, ref in ((place_ref[4], near_ref), (1 - place_ref[4], far_ref)):
        for k in range(count):
            z, y = divmod(k, 4)
            span = lanes((2 * y + c) * 4 + z, width)
            pseudo = ref[k]
            moment = outer_momentum * m_ref[:, span] + pseudo
            moment_ref[:, span] = moment
            theta_ref[:, span] = g_ref[:, span] - outer_rate * (pseudo + outer_momentum * moment)


def body(queries, keys, values, d_out, lengths, steps, theta_global, theta_local, momentum):
    rows = queries.shape[1]
    ranks, islands = lax.axis_size("fsdp"), lax.axis_size("island")
    rank = lax.axis_index("fsdp").astype(jnp.int32)
    me = lax.axis_index("island").astype(jnp.int32)
    place = jnp.stack([rank // 2, rank % 2, lengths[0], me % 8, me % 2])

    def along(x, r):
        return x if r == 0 else lax.ppermute(x, "fsdp", [(i, (i + 2 * r) % ranks) for i in range(ranks)])

    def back(blocks):
        return [along(x, -r) for r, x in enumerate(blocks)]

    def across(x):
        return lax.ppermute(x, "fsdp", [(i, i ^ 1) for i in range(ranks)])

    over_y_core = [[8 * z + i for i in range(8)] for z in range(4)]
    over_z = [[8 * z + i for z in range(4)] for i in range(8)]
    over_z_y = [[8 * z + 2 * y + c for z in range(4) for y in range(4)] for c in range(2)]

    def spread(x, groups):
        return lax.all_to_all(x, "island", 0, 0, axis_index_groups=groups, tiled=True)

    frag_rows, frag_width = theta_global.shape
    line, piece = frag_width // 8, frag_width // 32
    note = jnp.stack([steps[0], lengths[0] // 16, lengths[0] % 16]).astype(bf16)
    note = jnp.broadcast_to(jnp.pad(note, (0, NOTE - 3))[:, None], (NOTE, line))

    *packed, sent = pack(place, keys[0], values[0], queries[0], d_out[0], theta_local[0], note)
    drift = spread(sent, over_y_core)
    near, blocks = [along(x, r) for r, x in enumerate(packed[:GROUPS])], packed[GROUPS:]
    blocks[1] = along(blocks[1], 1)
    near, blocks[1] = lax.optimization_barrier((near, blocks[1]))
    near = jnp.stack(near)
    far = across(near)
    blocks[2], blocks[3] = after(near, (blocks[2], blocks[3]))
    blocks[2], blocks[3] = along(blocks[2], 2), along(blocks[3], 3)
    drift, = call(theta_sum_kernel, place, [theta_global, drift], [((4, frag_rows + 8, piece), f32)])
    blocks, near, far = after(drift, (blocks, near, far))
    drift = spread(drift, over_z)

    *context, v_near, v_far, stat = forward_call(place, blocks, near, far)
    v_far, drift, context, stat = lax.optimization_barrier((v_far, drift, context, stat))
    v_got = across(v_far)
    context = back(context)
    pseudo, = call(theta_mean_kernel, place, [drift], [((16, frag_rows, piece), f32)])
    stat = after(pseudo, stat)
    pseudo = spread(pseudo, over_z_y)
    *d_queries, k_near, k_far = backward_call(place, blocks, near, far, stat)
    k_far, v_got, context, pseudo = lax.optimization_barrier((k_far, v_got, context, pseudo))
    k_got = across(k_far)
    d_queries = back(d_queries)
    context = after(d_queries, context)
    context, = unpack(place, context, 1)
    k_got, pseudo = after(context, (k_got, pseudo))
    grads = call(merge_kernel, place, [k_near, k_got, v_near, v_got], [((rows, 2 * HEAD), bf16)] * GROUPS)
    grads_in = back(grads)
    pseudo = after(grads[0], pseudo)
    theta_far = lax.ppermute(pseudo, "island", [(i, i ^ 1) for i in range(islands)])
    d_queries, = unpack(place, after(grads[0], d_queries), 1)
    theta_new, momentum_new = call(
        theta_update_kernel, place, [pseudo, after(d_queries, theta_far), theta_global, momentum],
        [((frag_rows, frag_width), f32)] * 2)
    d_keys, d_values = unpack(place, after(theta_new, grads_in), 2)
    return (context[None], d_queries[None], d_keys[None], d_values[None], theta_new, momentum_new)


def solution(mesh):
    seq = P("island", "fsdp", None)
    return jax.shard_map(
        body,
        mesh=mesh,
        in_specs=(seq, seq, seq, seq, P("island"), P("island"), P("fsdp", None), seq, P("fsdp", None)),
        out_specs=(seq, seq, seq, seq, P("fsdp", None), P("fsdp", None)),
        check_vma=False,
    )
```

time: 509 us -> 154 us (0.30)
  waiting for transfers between devices: 260 us -> 39.4 us
  matrix products: 90.7 us -> 0 us
  starting transfers between devices: 0.16 us -> 63 us
  blocking collectives: 60.7 us -> 0 us
  Pallas kernels: 0 us -> 41.5 us
  other arithmetic: 38.9 us -> 0.15 us
  local copies, waits for them, and re-layouts: 40.6 us -> 5.27 us
  between operations: 16.6 us -> 2.23 us
    all_gather x2 -> x0, waiting for transfers between devices: 148 us -> none  [the longest x1 75.8 us: body(): lax.all_gather(values, 'fsdp', axis=1, tiled=True)]
    reduce_scatter x1 -> x0, waiting for transfers between devices: 112 us -> none  [body(): lax.psum_scatter(jnp.concatenate((key_part.reshape(lax.axis_size('fsdp')...]
    dot_general x18 -> x0, matrix products: 90.7 us -> none  [the longest x4 25.6 us: group_pass(): jnp.einsum('gqk,kd->qgd', soft_group, value_group, preferred_element_type...]
    psum x1 -> x0, blocking collectives: 60.7 us -> none  [body(): weighted_sum, total_weight = lax.psum((drift_terms, weight), 'island')]
    pallas_call x0 -> x10, Pallas kernels: none -> 41.5 us  [call(): pl.pallas_call(kernel, in_specs=[pl.BlockSpec(memory_space=pltpu.SMEM)] +...]
    ppermute x0 -> x19, starting transfers between devices: none -> 39.6 us  [the longest x15 24.7 us: along(): lax.ppermute(x, 'fsdp', [(i, (i + 2 * r) % ranks) for i in range(ranks)])]
    ppermute x0 -> x19, waiting for transfers between devices: none -> 39.4 us  [the longest x15 21.5 us: along(): lax.ppermute(x, 'fsdp', [(i, (i + 2 * r) % ranks) for i in range(ranks)])]
    all_to_all x0 -> x3, starting transfers between devices: none -> 23.4 us  [spread(): lax.all_to_all(x, 'island', 0, 0, axis_index_groups=groups, tiled=True)]
  transfers between devices with their start and end apart: 4 -> 22, of which waited for: 3 -> 9; matrix products, arithmetic and copies ran while one was open for 30% -> 0% of each run, Pallas kernels for 0% -> 21%
where the time goes in v2:
time: 154 us; the launch traced here: 152 us
  starting transfers between devices  63 us (41%)
  Pallas kernels  41.5 us (27%)
  waiting for transfers between devices  39.4 us (26%)
  local copies, waits for them, and re-layouts  5.27 us (3%)
  between operations  2.23 us (1%)
    pallas_call x10, Pallas kernels, call(): pl.pallas_call(kernel, in_specs=[pl.BlockSpec(memory_space=pltpu.SMEM)] +...  41.5 us
    ppermute x15, starting transfers between devices, along(): lax.ppermute(x, 'fsdp', [(i, (i + 2 * r) % ranks) for i in range(ranks)])  24.7 us
    all_to_all x3, starting transfers between devices, spread(): lax.all_to_all(x, 'island', 0, 0, axis_index_groups=groups, tiled=True)  23.4 us
    ppermute x15, waiting for transfers between devices, along(): lax.ppermute(x, 'fsdp', [(i, (i + 2 * r) % ranks) for i in range(ranks)])  21.5 us
    ppermute x3, waiting for transfers between devices, across(): return lax.ppermute(x, 'fsdp', [(i, i ^ 1) for i in range(ranks)])  17.9 us
    ppermute x3, starting transfers between devices, across(): return lax.ppermute(x, 'fsdp', [(i, i ^ 1) for i in range(ranks)])  14.8 us
    unnamed x54, local copies, waits for them, and re-layouts  3.93 us
  transfers between devices with their start and end apart: 22, of which 9 were waited for; matrix products, arithmetic and copies ran while one was open for 0% of the time, Pallas kernels for 21%

profile of v2, /device:TPU:16, one launch (start us, length us, event | category | flops | bytes accessed | tf_op | source)
XLA Modules:
  0.0 151.6 jit_solution(16116011062642598397)
XLA Ops:
  3.4 4.0 %shard_map.136 = (bf16[256,256]{1,0:T(8,128)(2,1)}, bf16[256,256]{1,0:T(8,128)(2,1)}, bf16[256,256]{1,0:T(8,128)(2,1)}, bf16[256,256]{1,0:T(8,128)(2,1)}, bf16[2...) custom-call(s32[5]{0:T(128)} %stack.46.place_ref, ...), custom_call_target="tpu_custom_call" | custom-call | tf_op jit(solution)/shard_map/pallas_call | solution.py:31
  7.4 1.6 %collective-permute-start.3 = (bf16[256,1024]{1,0:T(8,128)(2,1)}, bf16[256,1024]{1,0:T(8,128)(2,1)S(1)}, u32[]{:S(2)}, u32[]{:S(2)}) collective-permute-start(bf16[256,1024]{1,0:T(8,128)(2,1)} %get-tuple-element.86), channel_id=1, source_target_pairs={{0,2},{1,3},{2,4},{3,5},{4,6},{5,7},{6,0},{7,1},{8,10},{9,11},{10,... | collective-permute-start | bytes 1572872 | tf_op jit(solution)/shard_map/ppermute | solution.py:300
  9.0 4.8 %all-to-all-start = ((bf16[8,112,512]{2,1,0:T(8,128)(2,1)}), bf16[8,112,512]{2,1,0:T(8,128)(2,1)S(1)}, u32[]{:S(2)}, u32[]{:S(2)}) async-start(bf16[8,112,512]{2,1,0:T(8,128)(2,1)} %get-tuple-element.80), calls=%async_computation | async-start | bytes 1835008 | tf_op jit(solution)/shard_map/all_to_all | solution.py:313
  13.8 1.5 collective-permute-start
  15.3 2.5 %collective-permute-start.1 = (bf16[256,256]{1,0:T(8,128)(2,1)S(1)}, bf16[256,256]{1,0:T(8,128)(2,1)S(1)}, u32[]{:S(2)}, u32[]{:S(2)}) collective-permute-start(bf16[256,256]{1,0:T(8,128)(2,1)S(1)} %copy-done.25), channel_id=1, source_target_pairs={{0,4},{1,5},{2,6},{3,7},{4,0},{5,1},{6,2},{7,3},{8,12},{9,13},{10,... | collective-permute-start | bytes 393224 | tf_op jit(solution)/shard_map/ppermute | solution.py:300
  17.8 1.4 collective-permute-start.2
  19.2 6.4 %collective-permute-done = bf16[256,256]{1,0:T(8,128)(2,1)S(1)} collective-permute-done((bf16[256,256]{1,0:T(8,128)(2,1)S(1)}, bf16[256,256]{1,0:T(8,128)(2,1)S(1)}, u32[]{:S(2)}, u32[]{:S(2)}) %collective-permute-start) | collective-permute-done | bytes 131104 | tf_op jit(solution)/shard_map/ppermute | solution.py:300
  25.6 3.6 %collective-permute-done.1 = bf16[256,256]{1,0:T(8,128)(2,1)S(1)} collective-permute-done((bf16[256,256]{1,0:T(8,128)(2,1)S(1)}, bf16[256,256]{1,0:T(8,128)(2,1)S(1)}, u32[]{:S(2)}, u32[]{:S(2)}) %collective-permute-start.1) | collective-permute-done | bytes 131104 | tf_op jit(solution)/shard_map/ppermute | solution.py:300
  30.2 7.2 %collective-permute-start.6 = (bf16[4,256,256]{2,1,0:T(8,128)(2,1)S(1)}, bf16[4,256,256]{2,1,0:T(8,128)(2,1)}, u32[]{:S(2)}, u32[]{:S(2)}) collective-permute-start(bf16[4,256,256]{2,1,0:T(8,128)(2,1)S(1)} %pad_maximum_fusion.refs_4_), channel_id=1, source_target_pairs={{0,1},{1,0},{2,3},{3,2},{4,5},{5,4},{6,7},{7,6},{8,9},{9,8},{10,11... | collective-permute-start | bytes 1572872 | tf_op jit(solution)/shard_map/ppermute | solution.py:306
  38.3 2.6 %shard_map.137 = f32[4,104,128]{2,1,0:T(8,128)} custom-call(s32[5]{0:T(128)} %stack.46.place_ref, f32[96,4096]{1,0:T(8,128)} %g_ref.3, bf16[8,112,512]{2,1,0:T(8,128)(2,1)} %copy-done), custom_call_target="tpu_custom_call" | custom-call | tf_op jit(solution)/shard_map/pallas_call | solution.py:31
  40.9 3.4 %all-to-all-start.1 = ((f32[4,104,128]{2,1,0:T(8,128)}), f32[4,104,128]{2,1,0:T(8,128)S(1)}, u32[]{:S(2)}, u32[]{:S(2)}) async-start(f32[4,104,128]{2,1,0:T(8,128)} %shard_map.137), calls=%async_computation.1 | async-start | bytes 425984 | tf_op jit(solution)/shard_map/all_to_all | solution.py:313
  44.4 6.1 %collective-permute-done.5.refs_3_ = bf16[256,1024]{1,0:T(8,128)(2,1)S(1)} collective-permute-done((bf16[256,1024]{1,0:T(8,128)(2,1)}, bf16[256,1024]{1,0:T(8,128)(2,1)S(1)}, u32[]{:S(2)}, u32[]{:S(2)}) %collective-permute-start.5) | collective-permute-done | bytes 524320 | tf_op jit(solution)/shard_map/ppermute | solution.py:300
  50.4 8.9 %collective-permute-done.6.refs_5_ = bf16[4,256,256]{2,1,0:T(8,128)(2,1)} collective-permute-done((bf16[4,256,256]{2,1,0:T(8,128)(2,1)S(1)}, bf16[4,256,256]{2,1,0:T(8,128)(2,1)}, u32[]{:S(2)}, u32[]{:S(2)}) %collective-permute-start.6) | collective-permute-done | bytes 524320 | tf_op jit(solution)/shard_map/ppermute | solution.py:306
  59.3 10.6 %shard_map.138 = (bf16[256,512]{1,0:T(8,128)(2,1)}, bf16[256,512]{1,0:T(8,128)(2,1)}, bf16[256,512]{1,0:T(8,128)(2,1)}, bf16[256,512]{1,0:T(8,128)(2,1)}, f32[4,...) custom-call(s32[5]{0:T(128)} %stack.46.place_ref, ...), custom_call_target="tpu_custom_call" | custom-call | flops 12000000000 | bytes 5111808 | tf_op jit(solution)/shard_map/pallas_call | solution.py:31
  70.7 1.9 %shard_map.139 = f32[16,96,128]{2,1,0:T(8,128)} custom-call(s32[5]{0:T(128)} %stack.46.place_ref, f32[4,104,128]{2,1,0:T(8,128)} %copy-done.2), custom_call_target="tpu_custom_call" | custom-call | tf_op jit(solution)/shard_map/pallas_call | solution.py:31
  72.6 15.2 %all-to-all-start.2 = ((f32[16,96,128]{2,1,0:T(8,128)}), f32[16,96,128]{2,1,0:T(8,128)S(1)}, u32[]{:S(2)}, u32[]{:S(2)}) async-start(f32[16,96,128]{2,1,0:T(8,128)} %shard_map.139), calls=%async_computation.2 | async-start | bytes 1572864 | tf_op jit(solution)/shard_map/all_to_all | solution.py:313
  87.8 5.4 %collective-permute-start.10 = (bf16[4,256,128]{2,1,0:T(8,128)(2,1)S(1)}, bf16[4,256,128]{2,1,0:T(8,128)(2,1)S(1)}, u32[]{:S(2)}, u32[]{:S(2)}) collective-permute-start(bf16[4,256,128]{2,1,0:T(8,128)(2,1)S(1)} %copy-done.23), channel_id=1, source_target_pairs={{0,1},{1,0},{2,3},{3,2},{4,5},{5,4},{6,7},{7,6},{8,9},{9,8},{10,11... | collective-permute-start | bytes 786440 | tf_op jit(solution)/shard_map/ppermute | solution.py:306
  93.1 3.3 %collective-permute-start.11 = (bf16[256,512]{1,0:T(8,128)(2,1)S(1)}, bf16[256,512]{1,0:T(8,128)(2,1)S(1)}, u32[]{:S(2)}, u32[]{:S(2)}) collective-permute-start(bf16[256,512]{1,0:T(8,128)(2,1)S(1)} %copy-done.22), channel_id=1, source_target_pairs={{0,6},{1,7},{2,0},{3,1},{4,2},{5,3},{6,4},{7,5},{8,14},{9,15},{10,... | collective-permute-start | bytes 786440 | tf_op jit(solution)/shard_map/ppermute | solution.py:300
  97.4 8.9 %shard_map.140 = (bf16[256,512]{1,0:T(8,128)(2,1)}, bf16[256,512]{1,0:T(8,128)(2,1)}, bf16[256,512]{1,0:T(8,128)(2,1)}, bf16[256,512]{1,0:T(8,128)(2,1)}, f32[4,...) custom-call(s32[5]{0:T(128)} %stack.46.place_ref, bf16[256,1024]{1,0:T(8,128)(2,1)} %get-tuple-element.96.refs_0_, ...), custom_call_target="tpu_custom_call" | custom-call | flops 12000000000 | bytes 5111808 | tf_op jit(solution)/shard_map/pallas_call | solution.py:31
  106.3 3.1 %collective-permute-start.7 = (bf16[256,512]{1,0:T(8,128)(2,1)}, bf16[256,512]{1,0:T(8,128)(2,1)S(1)}, u32[]{:S(2)}, u32[]{:S(2)}) collective-permute-start(bf16[256,512]{1,0:T(8,128)(2,1)} %get-tuple-element.112), channel_id=1, source_target_pairs={{0,6},{1,7},{2,0},{3,1},{4,2},{5,3},{6,4},{7,5},{8,14},{9,15},{10,... | collective-permute-start | bytes 786440 | tf_op jit(solution)/shard_map/ppermute | solution.py:300
  109.4 4.9 %collective-permute-done.10.dv_far = bf16[4,256,128]{2,1,0:T(8,128)(2,1)S(1)} collective-permute-done((bf16[4,256,128]{2,1,0:T(8,128)(2,1)S(1)}, bf16[4,256,128]{2,1,0:T(8,128)(2,1)S(1)}, u32[]{:S(2)}, u32[]{:S(2)}) %collective-permute-start.10) | collective-permute-done | bytes 262176 | tf_op jit(solution)/shard_map/ppermute | solution.py:306
  114.3 2.7 %collective-permute-start.8 = (bf16[256,512]{1,0:T(8,128)(2,1)}, bf16[256,512]{1,0:T(8,128)(2,1)S(1)}, u32[]{:S(2)}, u32[]{:S(2)}) collective-permute-start(bf16[256,512]{1,0:T(8,128)(2,1)} %get-tuple-element.113), channel_id=1, source_target_pairs={{0,4},{1,5},{2,6},{3,7},{4,0},{5,1},{6,2},{7,3},{8,12},{9,13},{10,... | collective-permute-start | bytes 786440 | tf_op jit(solution)/shard_map/ppermute | solution.py:300
  118.1 2.3 %collective-permute-start.14 = (bf16[4,256,128]{2,1,0:T(8,128)(2,1)}, bf16[4,256,128]{2,1,0:T(8,128)(2,1)S(1)}, u32[]{:S(2)}, u32[]{:S(2)}) collective-permute-start(bf16[4,256,128]{2,1,0:T(8,128)(2,1)} %get-tuple-element.130), channel_id=1, source_target_pairs={{0,1},{1,0},{2,3},{3,2},{4,5},{5,4},{6,7},{7,6},{8,9},{9,8},{10,11... | collective-permute-start | bytes 786440 | tf_op jit(solution)/shard_map/ppermute | solution.py:306
  120.4 2.0 %collective-permute-done.8.refs_2_ = bf16[256,512]{1,0:T(8,128)(2,1)S(1)} collective-permute-done((bf16[256,512]{1,0:T(8,128)(2,1)}, bf16[256,512]{1,0:T(8,128)(2,1)S(1)}, u32[]{:S(2)}, u32[]{:S(2)}) %collective-permute-start.8) | collective-permute-done | bytes 262176 | tf_op jit(solution)/shard_map/ppermute | solution.py:300
  122.4 2.8 %collective-permute-done.9.refs_3_ = bf16[256,512]{1,0:T(8,128)(2,1)S(1)} collective-permute-done((bf16[256,512]{1,0:T(8,128)(2,1)}, bf16[256,512]{1,0:T(8,128)(2,1)S(1)}, u32[]{:S(2)}, u32[]{:S(2)}) %collective-permute-start.9) | collective-permute-done | bytes 262176 | tf_op jit(solution)/shard_map/ppermute | solution.py:300
  125.2 2.3 %shard_map.141 = bf16[256,2048]{1,0:T(8,128)(2,1)} custom-call(s32[5]{0:T(128)} %stack.46.place_ref, bf16[256,512]{1,0:T(8,128)(2,1)} %get-tuple-element.125.refs_0_, bf16[256,512]{1,0:T(8,128)(2,1)} %copy-done.7, bf16[256,512]{1,0:T(8,128)(2,1)} %copy-done.8, bf16[256,512]{1,0:T(8,128)(2,1)} %copy-done.10), custom_call_target="tpu_custom_call" | custom-call | tf_op jit(solution)/shard_map/pallas_call | solution.py:31
  127.6 4.1 %collective-permute-done.14.dk_far = bf16[4,256,128]{2,1,0:T(8,128)(2,1)S(1)} collective-permute-done((bf16[4,256,128]{2,1,0:T(8,128)(2,1)}, bf16[4,256,128]{2,1,0:T(8,128)(2,1)S(1)}, u32[]{:S(2)}, u32[]{:S(2)}) %collective-permute-start.14) | collective-permute-done | bytes 262176 | tf_op jit(solution)/shard_map/ppermute | solution.py:306
  132.4 2.2 %shard_map.142 = (bf16[256,256]{1,0:T(8,128)(2,1)}, bf16[256,256]{1,0:T(8,128)(2,1)}, bf16[256,256]{1,0:T(8,128)(2,1)}, bf16[256,256]{1,0:T(8,128)(2,1)}) custom-call(s32[5]{0:T(128)} %stack.46.place_ref, f32[4,256,128]{2,1,0:T(8,128)} %get-tuple-element.129.dk_near, bf16[4,256,128]{2,1,0:T(8,128)(2,1)} %copy-done.12, ...), custom_call_target="tpu_custom_call" | custom-call | tf_op jit(solution)/shard_map/pallas_call | solution.py:31
  134.7 4.5 %collective-permute-start.16 = (bf16[256,256]{1,0:T(8,128)(2,1)}, bf16[256,256]{1,0:T(8,128)(2,1)S(1)}, u32[]{:S(2)}, u32[]{:S(2)}) collective-permute-start(bf16[256,256]{1,0:T(8,128)(2,1)} %get-tuple-element.144), channel_id=1, source_target_pairs={{0,6},{1,7},{2,0},{3,1},{4,2},{5,3},{6,4},{7,5},{8,14},{9,15},{10,... | collective-permute-start | bytes 393224 | tf_op jit(solution)/shard_map/ppermute | solution.py:300
  140.5 2.2 %shard_map.143 = bf16[256,2048]{1,0:T(8,128)(2,1)} custom-call(s32[5]{0:T(128)} %stack.46.place_ref, bf16[256,512]{1,0:T(8,128)(2,1)} %get-tuple-element.136.refs_0_, bf16[256,512]{1,0:T(8,128)(2,1)} %copy-done.5, bf16[256,512]{1,0:T(8,128)(2,1)} %copy-done.6, bf16[256,512]{1,0:T(8,128)(2,1)} %copy-done.9), custom_call_target="tpu_custom_call" | custom-call | tf_op jit(solution)/shard_map/pallas_call | solution.py:31
  143.6 4.8 %shard_map.144 = (f32[96,4096]{1,0:T(8,128)}, f32[96,4096]{1,0:T(8,128)}) custom-call(s32[5]{0:T(128)} %stack.46.place_ref, f32[16,96,128]{2,1,0:T(8,128)} %copy-done.1, f32[16,96,128]{2,1,0:T(8,128)} %copy-done.3, f32[96,4096]{1,0:T(8,128)} %g_ref.3, f32[96,4096]{1,0:T(8,128)} %m_ref.1), custom_call_target="tpu_custom_call" | custom-call | tf_op jit(solution)/shard_map/pallas_call | solution.py:31
  149.7 2.0 %shard_map.145 = (bf16[256,512]{1,0:T(8,128)(2,1)}, bf16[256,512]{1,0:T(8,128)(2,1)}) custom-call(s32[5]{0:T(128)} %stack.46.place_ref, bf16[256,256]{1,0:T(8,128)(2,1)} %get-tuple-element.147.refs_0_, bf16[256,256]{1,0:T(8,128)(2,1)} %copy-done.13, bf16[256,256]{1,0:T(8,128)(2,1)} %copy-done.14, bf16[256,256]{1,0:T(8,128)(2,1)} %copy-done.15), custom_call_target="tpu_custom_call" | custom-call | tf_op jit(solution)/shard_map/pallas_call | solution.py:31
  (80 shorter events, 10.3 us)
Async XLA Ops:
  7.4 21.8 %copy-start.16 = (bf16[256,256]{1,0:T(8,128)(2,1)S(1)}, bf16[256,256]{1,0:T(8,128)(2,1)}, u32[]{:S(2)}) copy-start(bf16[256,256]{1,0:T(8,128)(2,1)} %get-tuple-element.88) | copy-start | bytes 393220
  7.4 21.8 %collective-permute-start.3 = (bf16[256,1024]{1,0:T(8,128)(2,1)}, bf16[256,1024]{1,0:T(8,128)(2,1)S(1)}, u32[]{:S(2)}, u32[]{:S(2)}) collective-permute-start(bf16[256,1024]{1,0:T(8,128)(2,1)} %get-tuple-element.86), channel_id=1, source_target_pairs={{0,2},{1,3},{2,4},{3,5},{4,6},{5,7},{6,0},{7,1},{8,10},{9,11},{10,... | collective-permute-start | bytes 1572872 | tf_op jit(solution)/shard_map/ppermute | solution.py:300
  9.0 28.4 %all-to-all-start = ((bf16[8,112,512]{2,1,0:T(8,128)(2,1)}), bf16[8,112,512]{2,1,0:T(8,128)(2,1)S(1)}, u32[]{:S(2)}, u32[]{:S(2)}) async-start(bf16[8,112,512]{2,1,0:T(8,128)(2,1)} %get-tuple-element.80), calls=%async_computation | async-start | bytes 1835008 | tf_op jit(solution)/shard_map/all_to_all | solution.py:313
  13.8 11.8 %collective-permute-start = (bf16[256,256]{1,0:T(8,128)(2,1)S(1)}, bf16[256,256]{1,0:T(8,128)(2,1)S(1)}, u32[]{:S(2)}, u32[]{:S(2)}) collective-permute-start(bf16[256,256]{1,0:T(8,128)(2,1)S(1)} %copy-done.26), channel_id=1, source_target_pairs={{0,2},{1,3},{2,4},{3,5},{4,6},{5,7},{6,0},{7,1},{8,10},{9,11},{10,... | collective-permute-start | bytes 393224 | tf_op jit(solution)/shard_map/ppermute | solution.py:300
  15.3 13.9 %collective-permute-start.1 = (bf16[256,256]{1,0:T(8,128)(2,1)S(1)}, bf16[256,256]{1,0:T(8,128)(2,1)S(1)}, u32[]{:S(2)}, u32[]{:S(2)}) collective-permute-start(bf16[256,256]{1,0:T(8,128)(2,1)S(1)} %copy-done.25), channel_id=1, source_target_pairs={{0,4},{1,5},{2,6},{3,7},{4,0},{5,1},{6,2},{7,3},{8,12},{9,13},{10,... | collective-permute-start | bytes 393224 | tf_op jit(solution)/shard_map/ppermute | solution.py:300
  17.8 11.4 %collective-permute-start.2 = (bf16[256,256]{1,0:T(8,128)(2,1)S(1)}, bf16[256,256]{1,0:T(8,128)(2,1)S(1)}, u32[]{:S(2)}, u32[]{:S(2)}) collective-permute-start(bf16[256,256]{1,0:T(8,128)(2,1)S(1)} %copy-done.24), channel_id=1, source_target_pairs={{0,6},{1,7},{2,0},{3,1},{4,2},{5,3},{6,4},{7,5},{8,14},{9,15},{10,... | collective-permute-start | bytes 393224 | tf_op jit(solution)/shard_map/ppermute | solution.py:300
  29.3 30.0 %copy-start.4 = (bf16[4,256,256]{2,1,0:T(8,128)(2,1)}, bf16[4,256,256]{2,1,0:T(8,128)(2,1)S(1)}, u32[]{:S(2)}) copy-start(bf16[4,256,256]{2,1,0:T(8,128)(2,1)S(1)} %pad_maximum_fusion.refs_4_) | copy-start | bytes 1572868
  29.3 15.0 %collective-permute-start.4 = (bf16[256,1024]{1,0:T(8,128)(2,1)}, bf16[256,1024]{1,0:T(8,128)(2,1)S(1)}, u32[]{:S(2)}, u32[]{:S(2)}) collective-permute-start(bf16[256,1024]{1,0:T(8,128)(2,1)} %get-tuple-element.94), channel_id=1, source_target_pairs={{0,4},{1,5},{2,6},{3,7},{4,0},{5,1},{6,2},{7,3},{8,12},{9,13},{10,... | collective-permute-start | bytes 1572872 | tf_op jit(solution)/shard_map/ppermute | solution.py:300
  30.2 20.2 %collective-permute-start.5 = (bf16[256,1024]{1,0:T(8,128)(2,1)}, bf16[256,1024]{1,0:T(8,128)(2,1)S(1)}, u32[]{:S(2)}, u32[]{:S(2)}) collective-permute-start(bf16[256,1024]{1,0:T(8,128)(2,1)} %get-tuple-element.95), channel_id=1, source_target_pairs={{0,6},{1,7},{2,0},{3,1},{4,2},{5,3},{6,4},{7,5},{8,14},{9,15},{10,... | collective-permute-start | bytes 1572872 | tf_op jit(solution)/shard_map/ppermute | solution.py:300
  30.2 29.1 %collective-permute-start.6 = (bf16[4,256,256]{2,1,0:T(8,128)(2,1)S(1)}, bf16[4,256,256]{2,1,0:T(8,128)(2,1)}, u32[]{:S(2)}, u32[]{:S(2)}) collective-permute-start(bf16[4,256,256]{2,1,0:T(8,128)(2,1)S(1)} %pad_maximum_fusion.refs_4_), channel_id=1, source_target_pairs={{0,1},{1,0},{2,3},{3,2},{4,5},{5,4},{6,7},{7,6},{8,9},{9,8},{10,11... | collective-permute-start | bytes 1572872 | tf_op jit(solution)/shard_map/ppermute | solution.py:306
  40.9 29.0 %all-to-all-start.1 = ((f32[4,104,128]{2,1,0:T(8,128)}), f32[4,104,128]{2,1,0:T(8,128)S(1)}, u32[]{:S(2)}, u32[]{:S(2)}) async-start(f32[4,104,128]{2,1,0:T(8,128)} %shard_map.137), calls=%async_computation.1 | async-start | bytes 425984 | tf_op jit(solution)/shard_map/all_to_all | solution.py:313
  44.3 15.0 %copy-start.18 = (bf16[256,1024]{1,0:T(8,128)(2,1)}, bf16[256,1024]{1,0:T(8,128)(2,1)S(1)}, u32[]{:S(2)}) copy-start(bf16[256,1024]{1,0:T(8,128)(2,1)S(1)} %collective-permute-done.4.refs_2_) | copy-start | bytes 1572868
  69.9 17.9 %copy-start.23 = (bf16[4,256,128]{2,1,0:T(8,128)(2,1)S(1)}, bf16[4,256,128]{2,1,0:T(8,128)(2,1)}, u32[]{:S(2)}) copy-start(bf16[4,256,128]{2,1,0:T(8,128)(2,1)} %get-tuple-element.116) | copy-start | bytes 786436
  69.9 23.2 %copy-start.22 = (bf16[256,512]{1,0:T(8,128)(2,1)S(1)}, bf16[256,512]{1,0:T(8,128)(2,1)}, u32[]{:S(2)}) copy-start(bf16[256,512]{1,0:T(8,128)(2,1)} %get-tuple-element.118) | copy-start | bytes 786436
  69.9 26.5 %copy-start.21 = (bf16[256,512]{1,0:T(8,128)(2,1)S(1)}, bf16[256,512]{1,0:T(8,128)(2,1)}, u32[]{:S(2)}) copy-start(bf16[256,512]{1,0:T(8,128)(2,1)} %get-tuple-element.119) | copy-start | bytes 786436
  69.9 27.3 %copy-start.20 = (bf16[256,512]{1,0:T(8,128)(2,1)S(1)}, bf16[256,512]{1,0:T(8,128)(2,1)}, u32[]{:S(2)}) copy-start(bf16[256,512]{1,0:T(8,128)(2,1)} %get-tuple-element.120) | copy-start | bytes 786436
  72.6 45.6 %all-to-all-start.2 = ((f32[16,96,128]{2,1,0:T(8,128)}), f32[16,96,128]{2,1,0:T(8,128)S(1)}, u32[]{:S(2)}, u32[]{:S(2)}) async-start(f32[16,96,128]{2,1,0:T(8,128)} %shard_map.139), calls=%async_computation.2 | async-start | bytes 1572864 | tf_op jit(solution)/shard_map/all_to_all | solution.py:313
  87.8 26.5 %collective-permute-start.10 = (bf16[4,256,128]{2,1,0:T(8,128)(2,1)S(1)}, bf16[4,256,128]{2,1,0:T(8,128)(2,1)S(1)}, u32[]{:S(2)}, u32[]{:S(2)}) collective-permute-start(bf16[4,256,128]{2,1,0:T(8,128)(2,1)S(1)} %copy-done.23), channel_id=1, source_target_pairs={{0,1},{1,0},{2,3},{3,2},{4,5},{5,4},{6,7},{7,6},{8,9},{9,8},{10,11... | collective-permute-start | bytes 786440 | tf_op jit(solution)/shard_map/ppermute | solution.py:306
  93.1 23.9 %collective-permute-start.11 = (bf16[256,512]{1,0:T(8,128)(2,1)S(1)}, bf16[256,512]{1,0:T(8,128)(2,1)S(1)}, u32[]{:S(2)}, u32[]{:S(2)}) collective-permute-start(bf16[256,512]{1,0:T(8,128)(2,1)S(1)} %copy-done.22), channel_id=1, source_target_pairs={{0,6},{1,7},{2,0},{3,1},{4,2},{5,3},{6,4},{7,5},{8,14},{9,15},{10,... | collective-permute-start | bytes 786440 | tf_op jit(solution)/shard_map/ppermute | solution.py:300
  96.4 21.7 %collective-permute-start.12 = (bf16[256,512]{1,0:T(8,128)(2,1)S(1)}, bf16[256,512]{1,0:T(8,128)(2,1)S(1)}, u32[]{:S(2)}, u32[]{:S(2)}) collective-permute-start(bf16[256,512]{1,0:T(8,128)(2,1)S(1)} %copy-done.21), channel_id=1, source_target_pairs={{0,4},{1,5},{2,6},{3,7},{4,0},{5,1},{6,2},{7,3},{8,12},{9,13},{10,... | collective-permute-start | bytes 786440 | tf_op jit(solution)/shard_map/ppermute | solution.py:300
  97.2 20.9 %collective-permute-start.13 = (bf16[256,512]{1,0:T(8,128)(2,1)S(1)}, bf16[256,512]{1,0:T(8,128)(2,1)S(1)}, u32[]{:S(2)}, u32[]{:S(2)}) collective-permute-start(bf16[256,512]{1,0:T(8,128)(2,1)S(1)} %copy-done.20), channel_id=1, source_target_pairs={{0,2},{1,3},{2,4},{3,5},{4,6},{5,7},{6,0},{7,1},{8,10},{9,11},{10,... | collective-permute-start | bytes 786440 | tf_op jit(solution)/shard_map/ppermute | solution.py:300
  106.3 14.1 %collective-permute-start.7 = (bf16[256,512]{1,0:T(8,128)(2,1)}, bf16[256,512]{1,0:T(8,128)(2,1)S(1)}, u32[]{:S(2)}, u32[]{:S(2)}) collective-permute-start(bf16[256,512]{1,0:T(8,128)(2,1)} %get-tuple-element.112), channel_id=1, source_target_pairs={{0,6},{1,7},{2,0},{3,1},{4,2},{5,3},{6,4},{7,5},{8,14},{9,15},{10,... | collective-permute-start | bytes 786440 | tf_op jit(solution)/shard_map/ppermute | solution.py:300
  114.3 17.4 %copy-start.11 = (bf16[4,256,128]{2,1,0:T(8,128)(2,1)}, bf16[4,256,128]{2,1,0:T(8,128)(2,1)S(1)}, u32[]{:S(2)}) copy-start(bf16[4,256,128]{2,1,0:T(8,128)(2,1)S(1)} %collective-permute-done.10.dv_far) | copy-start | bytes 786436
  114.3 8.1 %collective-permute-start.8 = (bf16[256,512]{1,0:T(8,128)(2,1)}, bf16[256,512]{1,0:T(8,128)(2,1)S(1)}, u32[]{:S(2)}, u32[]{:S(2)}) collective-permute-start(bf16[256,512]{1,0:T(8,128)(2,1)} %get-tuple-element.113), channel_id=1, source_target_pairs={{0,4},{1,5},{2,6},{3,7},{4,0},{5,1},{6,2},{7,3},{8,12},{9,13},{10,... | collective-permute-start | bytes 786440 | tf_op jit(solution)/shard_map/ppermute | solution.py:300
  117.0 8.2 %collective-permute-start.9 = (bf16[256,512]{1,0:T(8,128)(2,1)}, bf16[256,512]{1,0:T(8,128)(2,1)S(1)}, u32[]{:S(2)}, u32[]{:S(2)}) collective-permute-start(bf16[256,512]{1,0:T(8,128)(2,1)} %get-tuple-element.114), channel_id=1, source_target_pairs={{0,2},{1,3},{2,4},{3,5},{4,6},{5,7},{6,0},{7,1},{8,10},{9,11},{10,... | collective-permute-start | bytes 786440 | tf_op jit(solution)/shard_map/ppermute | solution.py:300
  118.1 16.4 %copy-start.1 = (f32[16,96,128]{2,1,0:T(8,128)}, f32[16,96,128]{2,1,0:T(8,128)S(1)}, u32[]{:S(2)}) copy-start(f32[16,96,128]{2,1,0:T(8,128)S(1)} %all-to-all-done.2.near_ref) | copy-start | bytes 2359300
  118.1 13.5 %collective-permute-start.14 = (bf16[4,256,128]{2,1,0:T(8,128)(2,1)}, bf16[4,256,128]{2,1,0:T(8,128)(2,1)S(1)}, u32[]{:S(2)}, u32[]{:S(2)}) collective-permute-start(bf16[4,256,128]{2,1,0:T(8,128)(2,1)} %get-tuple-element.130), channel_id=1, source_target_pairs={{0,1},{1,0},{2,3},{3,2},{4,5},{5,4},{6,7},{7,6},{8,9},{9,8},{10,11... | collective-permute-start | bytes 786440 | tf_op jit(solution)/shard_map/ppermute | solution.py:306
  120.4 14.1 %copy-start.5 = (bf16[256,512]{1,0:T(8,128)(2,1)}, bf16[256,512]{1,0:T(8,128)(2,1)S(1)}, u32[]{:S(2)}) copy-start(bf16[256,512]{1,0:T(8,128)(2,1)S(1)} %collective-permute-done.7.refs_1_) | copy-start | bytes 786436
  134.6 8.1 %collective-permute-start.15 = (f32[16,96,128]{2,1,0:T(8,128)S(1)}, f32[16,96,128]{2,1,0:T(8,128)S(1)}, u32[]{:S(2)}, u32[]{:S(2)}) collective-permute-start(f32[16,96,128]{2,1,0:T(8,128)S(1)} %all-to-all-done.2.near_ref), channel_id=1, source_target_pairs={{0,8},{8,0},{16,24},{24,16},{32,40},{40,32},{48,56},{56,48},{64,72... | collective-permute-start | bytes 2359304 | tf_op jit(solution)/shard_map/ppermute | solution.py:350
  134.7 13.7 %collective-permute-start.16 = (bf16[256,256]{1,0:T(8,128)(2,1)}, bf16[256,256]{1,0:T(8,128)(2,1)S(1)}, u32[]{:S(2)}, u32[]{:S(2)}) collective-permute-start(bf16[256,256]{1,0:T(8,128)(2,1)} %get-tuple-element.144), channel_id=1, source_target_pairs={{0,6},{1,7},{2,0},{3,1},{4,2},{5,3},{6,4},{7,5},{8,14},{9,15},{10,... | collective-permute-start | bytes 393224 | tf_op jit(solution)/shard_map/ppermute | solution.py:300
  139.2 9.2 %collective-permute-start.17 = (bf16[256,256]{1,0:T(8,128)(2,1)}, bf16[256,256]{1,0:T(8,128)(2,1)S(1)}, u32[]{:S(2)}, u32[]{:S(2)}) collective-permute-start(bf16[256,256]{1,0:T(8,128)(2,1)} %get-tuple-element.145), channel_id=1, source_target_pairs={{0,4},{1,5},{2,6},{3,7},{4,0},{5,1},{6,2},{7,3},{8,12},{9,13},{10,... | collective-permute-start | bytes 393224 | tf_op jit(solution)/shard_map/ppermute | solution.py:300
  139.5 9.5 %collective-permute-start.18 = (bf16[256,256]{1,0:T(8,128)(2,1)}, bf16[256,256]{1,0:T(8,128)(2,1)S(1)}, u32[]{:S(2)}, u32[]{:S(2)}) collective-permute-start(bf16[256,256]{1,0:T(8,128)(2,1)} %get-tuple-element.146), channel_id=1, source_target_pairs={{0,2},{1,3},{2,4},{3,5},{4,6},{5,7},{6,0},{7,1},{8,10},{9,11},{10,... | collective-permute-start | bytes 393224 | tf_op jit(solution)/shard_map/ppermute | solution.py:300
  (17 other events, 94.4 us)

commit v3 on v2

--- a/solution.py
+++ b/solution.py
@@ -82,7 +82,7 @@
 def forward_kernel(place_ref, *refs):
     qg_refs, (near_ref, far_ref), refs = refs[:GROUPS], refs[GROUPS:GROUPS + 2], refs[GROUPS + 2:]
     ctx_refs, (near_out, far_out, stat_ref), refs = refs[:GROUPS], refs[GROUPS:GROUPS + 3], refs[GROUPS + 3:]
-    soft, q_cols, g_cols, g_rows, v_cols, kv_ref, dv_ref = refs
+    soft, q_cols, g_cols, g_rows, v_cols, kv_ref, dv_ref, acc = refs
     rows = qg_refs[0].shape[0]
     window = kv_ref.shape[0]
     wide = WIDE * rows
@@ -129,9 +129,12 @@
         def forward(j, context):
             p = (soft[at(j), :] * inverse).astype(bf16)
             dv_ref[at(j), :] += jnp.dot(p, g_rows[...], preferred_element_type=f32)
-            return context + jnp.dot(v_cols[:, at(j)], p, preferred_element_type=f32)
-
-        context = lax.fori_loop(0, live, forward, jnp.zeros((HEAD, wide), f32))
+            acc[...] += jnp.dot(v_cols[:, at(j)], p, preferred_element_type=f32)
+            return context
+
+        acc[...] = jnp.zeros_like(acc)
+        lax.fori_loop(0, live, forward, 0)
+        context = acc[...]
         stat_ref[r, 0:1, :] = top
         stat_ref[r, 1:2, :] = inverse
         stat_ref[r, 2:3, :] = jnp.sum(g_cols[...].astype(f32) * context, axis=0, keepdims=True)
@@ -200,7 +203,7 @@
         forward_kernel, place, [*blocks, near, far],
         [((rows, COLS), bf16)] * groups + [near_part, far_part, ((groups, 8, wide), f32)],
         [((window, wide), f32), ((HEAD, wide), bf16), ((HEAD, wide), bf16), ((wide, HEAD), bf16), ((HEAD, window), bf16),
-         ((window, 2 * HEAD), bf16), ((window, HEAD), f32)],
+         ((window, 2 * HEAD), bf16), ((window, HEAD), f32), ((HEAD, wide), f32)],
         flops=12 * 10**9, exps=10**7, vmem=58)
 
 
@@ -216,24 +219,36 @@
         flops=12 * 10**9, exps=10**7, vmem=58)
 
 
-def pack_kernel(place_ref, k_ref, v_ref, q_ref, g_ref, local_ref, note_ref, *refs):
-    pair_refs, block_refs, sent_ref = refs[:GROUPS], refs[GROUPS:2 * GROUPS], refs[2 * GROUPS]
-    for out_refs, ins, width in ((pair_refs, (k_ref, v_ref), HEAD), (block_refs, (q_ref, g_ref), COLS)):
-        for r in range(GROUPS):
-            for i, ref in enumerate(ins):
-                out_refs[r][:, i * width:(i + 1) * width] = ref[:, lanes((place_ref[0] + r) % GROUPS, width)]
+def pack_pairs_kernel(place_ref, a_ref, b_ref, *out_refs):
+    width = a_ref.shape[1] // GROUPS
+    for r in range(GROUPS):
+        span = lanes((place_ref[0] + r) % GROUPS, width)
+        out_refs[r][:, :width] = a_ref[:, span]
+        out_refs[r][:, width:] = b_ref[:, span]
+
+
+def pack_kernel(place_ref, q_ref, g_ref, local_ref, *refs):
+    out_refs, sent_ref = refs[:GROUPS], refs[GROUPS]
+    pack_pairs_kernel(place_ref, q_ref, g_ref, *out_refs)
     width = sent_ref.shape[2]
+    row = lax.broadcasted_iota(jnp.int32, (NOTE, width), 0)
+    length, steps = place_ref[2], place_ref[5]
+    note = jnp.where(row == 0, steps, jnp.where(row == 1, length // 16, length % 16)).astype(f32).astype(bf16)
     for i in range(sent_ref.shape[0]):
         sent_ref[i, :-NOTE, :] = local_ref[:, i * width:(i + 1) * width]
-        sent_ref[i, -NOTE:, :] = note_ref[...]
-
-
-def pack(place, k, v, q, g, local, note):
-    rows, (note_rows, line) = k.shape[0], note.shape
+        sent_ref[i, -NOTE:, :] = note
+
+
+def pack_pairs(place, k, v):
+    rows, width = k.shape
+    return call(pack_pairs_kernel, place, [k, v], [((rows, 2 * width // GROUPS), bf16)] * GROUPS)
+
+
+def pack(place, q, g, local):
+    rows, (frag_rows, frag_width) = q.shape[0], local.shape
     return call(
-        pack_kernel, place, [k, v, q, g, local, note],
-        [((rows, 2 * HEAD), bf16)] * GROUPS + [((rows, 2 * COLS), bf16)] * GROUPS
-        + [((local.shape[1] // line, local.shape[0] + note_rows, line), bf16)])
+        pack_kernel, place, [q, g, local],
+        [((rows, 2 * COLS), bf16)] * GROUPS + [((8, frag_rows + NOTE, frag_width // 8), bf16)])
 
 
 def unpack_kernel(place_ref, *refs):
@@ -294,7 +309,7 @@
     ranks, islands = lax.axis_size("fsdp"), lax.axis_size("island")
     rank = lax.axis_index("fsdp").astype(jnp.int32)
     me = lax.axis_index("island").astype(jnp.int32)
-    place = jnp.stack([rank // 2, rank % 2, lengths[0], me % 8, me % 2])
+    place = jnp.stack([rank // 2, rank % 2, lengths[0], me % 8, me % 2, steps[0]])
 
     def along(x, r):
         return x if r == 0 else lax.ppermute(x, "fsdp", [(i, (i + 2 * r) % ranks) for i in range(ranks)])
@@ -314,18 +329,13 @@
 
     frag_rows, frag_width = theta_global.shape
     line, piece = frag_width // 8, frag_width // 32
-    note = jnp.stack([steps[0], lengths[0] // 16, lengths[0] % 16]).astype(bf16)
-    note = jnp.broadcast_to(jnp.pad(note, (0, NOTE - 3))[:, None], (NOTE, line))
-
-    *packed, sent = pack(place, keys[0], values[0], queries[0], d_out[0], theta_local[0], note)
-    drift = spread(sent, over_y_core)
-    near, blocks = [along(x, r) for r, x in enumerate(packed[:GROUPS])], packed[GROUPS:]
-    blocks[1] = along(blocks[1], 1)
-    near, blocks[1] = lax.optimization_barrier((near, blocks[1]))
+    near = [along(x, r) for r, x in enumerate(pack_pairs(place, keys[0], values[0]))]
+    near, queries, d_out, theta_local = lax.optimization_barrier((near, queries, d_out, theta_local))
     near = jnp.stack(near)
     far = across(near)
-    blocks[2], blocks[3] = after(near, (blocks[2], blocks[3]))
-    blocks[2], blocks[3] = along(blocks[2], 2), along(blocks[3], 3)
+    *blocks, sent = pack(place, queries[0], d_out[0], theta_local[0])
+    blocks = [along(x, r) for r, x in enumerate(blocks)]
+    drift = spread(sent, over_y_core)
     drift, = call(theta_sum_kernel, place, [theta_global, drift], [((4, frag_rows + 8, piece), f32)])
     blocks, near, far = after(drift, (blocks, near, far))
     drift = spread(drift, over_z)

time: 154 us -> 152 us (0.987)
  waiting for transfers between devices: 39.4 us -> 37.5 us
    ppermute x3, waiting for transfers between devices: 17.9 us -> 13.4 us  [across(): return lax.ppermute(x, 'fsdp', [(i, i ^ 1) for i in range(ranks)])]
    ppermute x3, starting transfers between devices: 14.8 us -> 12.6 us  [across(): return lax.ppermute(x, 'fsdp', [(i, i ^ 1) for i in range(ranks)])]
    ppermute x15, waiting for transfers between devices: 21.5 us -> 23.4 us  [along(): lax.ppermute(x, 'fsdp', [(i, (i + 2 * r) % ranks) for i in range(ranks)])]
    pallas_call x10 -> x11, Pallas kernels: 41.5 us -> 42.6 us  [call(): pl.pallas_call(kernel, in_specs=[pl.BlockSpec(memory_space=pltpu.SMEM)] +...]
    unnamed x54 -> x48, local copies, waits for them, and re-layouts: 3.93 us -> 4.46 us
  transfers between devices with their start and end apart: 22 -> 22, of which waited for: 9 -> 12; matrix products, arithmetic and copies ran while one was open for 0% -> 0% of each run, Pallas kernels for 21% -> 21%
where the time goes in v3:
time: 152 us; the launch traced here: 149 us
  starting transfers between devices  62.1 us (41%)
  Pallas kernels  42.6 us (28%)
  waiting for transfers between devices  37.5 us (25%)
  local copies, waits for them, and re-layouts  5.09 us (3%)
  between operations  2.11 us (1%)
    pallas_call x11, Pallas kernels, call(): pl.pallas_call(kernel, in_specs=[pl.BlockSpec(memory_space=pltpu.SMEM)] +...  42.6 us
    ppermute x15, starting transfers between devices, along(): lax.ppermute(x, 'fsdp', [(i, (i + 2 * r) % ranks) for i in range(ranks)])  25.7 us
    all_to_all x3, starting transfers between devices, spread(): lax.all_to_all(x, 'island', 0, 0, axis_index_groups=groups, tiled=True)  23.6 us
    ppermute x15, waiting for transfers between devices, along(): lax.ppermute(x, 'fsdp', [(i, (i + 2 * r) % ranks) for i in range(ranks)])  23.4 us
    ppermute x3, waiting for transfers between devices, across(): return lax.ppermute(x, 'fsdp', [(i, i ^ 1) for i in range(ranks)])  13.4 us
    ppermute x3, starting transfers between devices, across(): return lax.ppermute(x, 'fsdp', [(i, i ^ 1) for i in range(ranks)])  12.6 us
    unnamed x48, local copies, waits for them, and re-layouts  4.46 us
  transfers between devices with their start and end apart: 22, of which 12 were waited for; matrix products, arithmetic and copies ran while one was open for 0% of the time, Pallas kernels for 21%

profile of v3, /device:TPU:16, one launch (start us, length us, event | category | flops | bytes accessed | tf_op | source)
XLA Modules:
  0.0 149.5 jit_solution(1626408501342830892)
XLA Ops:
  2.6 1.9 %shard_map.136 = (bf16[256,256]{1,0:T(8,128)(2,1)}, bf16[256,256]{1,0:T(8,128)(2,1)}, bf16[256,256]{1,0:T(8,128)(2,1)}, bf16[256,256]{1,0:T(8,128)(2,1)}) custom-call(s32[6]{0:T(128)} %stack.34.place_ref, bf16[256,512]{1,0:T(8,128)(2,1)} %bitcast.22, bf16[256,512]{1,0:T(8,128)(2,1)} %bitcast.23), custom_call_target="tpu_custom_call" | custom-call | tf_op jit(solution)/shard_map/pallas_call | solution.py:31
  4.5 1.5 collective-permute-start
  6.0 2.7 %collective-permute-start.1 = (bf16[256,256]{1,0:T(8,128)(2,1)}, bf16[256,256]{1,0:T(8,128)(2,1)S(1)}, u32[]{:S(2)}, u32[]{:S(2)}) collective-permute-start(bf16[256,256]{1,0:T(8,128)(2,1)} %get-tuple-element.82), channel_id=1, source_target_pairs={{0,4},{1,5},{2,6},{3,7},{4,0},{5,1},{6,2},{7,3},{8,12},{9,13},{10,... | collective-permute-start | bytes 393224 | tf_op jit(solution)/shard_map/ppermute | solution.py:315
  11.3 3.6 %collective-permute-done.1 = bf16[256,256]{1,0:T(8,128)(2,1)S(1)} collective-permute-done((bf16[256,256]{1,0:T(8,128)(2,1)}, bf16[256,256]{1,0:T(8,128)(2,1)S(1)}, u32[]{:S(2)}, u32[]{:S(2)}) %collective-permute-start.1) | collective-permute-done | bytes 131104 | tf_op jit(solution)/shard_map/ppermute | solution.py:315
  14.9 3.6 %shard_map.137 = (bf16[256,1024]{1,0:T(8,128)(2,1)}, bf16[256,1024]{1,0:T(8,128)(2,1)}, bf16[256,1024]{1,0:T(8,128)(2,1)}, bf16[256,1024]{1,0:T(8,128)(2,1)}, bf16[8,112,512]{2,1,0:T(8,128)(2,1)}) custom-call(s32[6]{0:T(128)} %stack.34.place_ref, bf16[256,2048]{1,0:T(8,128)(2,1)} %bitcast.17, bf16[256,2048]{1,0:T(8,128)(2,1)} %bitcast.18, ...), custom_call_target="tpu_custom_call" | custom-call | tf_op jit(solution)/shard_map/pallas_call | solution.py:31
  18.5 4.9 %all-to-all-start = ((bf16[8,112,512]{2,1,0:T(8,128)(2,1)}), bf16[8,112,512]{2,1,0:T(8,128)(2,1)S(1)}, u32[]{:S(2)}, u32[]{:S(2)}) async-start(bf16[8,112,512]{2,1,0:T(8,128)(2,1)} %get-tuple-element.87), calls=%async_computation | async-start | bytes 1835008 | tf_op jit(solution)/shard_map/all_to_all | solution.py:328
  23.5 7.3 %collective-permute-start.6 = (bf16[4,256,256]{2,1,0:T(8,128)(2,1)S(1)}, bf16[4,256,256]{2,1,0:T(8,128)(2,1)S(1)}, u32[]{:S(2)}, u32[]{:S(2)}) collective-permute-start(bf16[4,256,256]{2,1,0:T(8,128)(2,1)S(1)} %pad_maximum_fusion.refs_4_), channel_id=1, source_target_pairs={{0,1},{1,0},{2,3},{3,2},{4,5},{5,4},{6,7},{7,6},{8,9},{9,8},{10,11... | collective-permute-start | bytes 1572872 | tf_op jit(solution)/shard_map/ppermute | solution.py:321
  32.1 2.4 %collective-permute-start.4 = (bf16[256,1024]{1,0:T(8,128)(2,1)}, bf16[256,1024]{1,0:T(8,128)(2,1)S(1)}, u32[]{:S(2)}, u32[]{:S(2)}) collective-permute-start(bf16[256,1024]{1,0:T(8,128)(2,1)} %get-tuple-element.90), channel_id=1, source_target_pairs={{0,4},{1,5},{2,6},{3,7},{4,0},{5,1},{6,2},{7,3},{8,12},{9,13},{10,... | collective-permute-start | bytes 1572872 | tf_op jit(solution)/shard_map/ppermute | solution.py:315
  34.5 1.5 %collective-permute-start.5 = (bf16[256,1024]{1,0:T(8,128)(2,1)}, bf16[256,1024]{1,0:T(8,128)(2,1)}, u32[]{:S(2)}, u32[]{:S(2)}) collective-permute-start(bf16[256,1024]{1,0:T(8,128)(2,1)} %get-tuple-element.91), channel_id=1, source_target_pairs={{0,6},{1,7},{2,0},{3,1},{4,2},{5,3},{6,4},{7,5},{8,14},{9,15},{10,... | collective-permute-start | bytes 1572872 | tf_op jit(solution)/shard_map/ppermute | solution.py:315
  37.0 2.6 %shard_map.138 = f32[4,104,128]{2,1,0:T(8,128)} custom-call(s32[6]{0:T(128)} %stack.34.place_ref, f32[96,4096]{1,0:T(8,128)} %g_ref.3, bf16[8,112,512]{2,1,0:T(8,128)(2,1)} %copy-done), custom_call_target="tpu_custom_call" | custom-call | tf_op jit(solution)/shard_map/pallas_call | solution.py:31
  39.6 4.6 %all-to-all-start.1 = ((f32[4,104,128]{2,1,0:T(8,128)}), f32[4,104,128]{2,1,0:T(8,128)S(1)}, u32[]{:S(2)}, u32[]{:S(2)}) async-start(f32[4,104,128]{2,1,0:T(8,128)} %shard_map.138), calls=%async_computation.1 | async-start | bytes 425984 | tf_op jit(solution)/shard_map/all_to_all | solution.py:328
  46.5 11.1 %collective-permute-done.4.refs_2_ = bf16[256,1024]{1,0:T(8,128)(2,1)S(1)} collective-permute-done((bf16[256,1024]{1,0:T(8,128)(2,1)}, bf16[256,1024]{1,0:T(8,128)(2,1)S(1)}, u32[]{:S(2)}, u32[]{:S(2)}) %collective-permute-start.4) | collective-permute-done | bytes 524320 | tf_op jit(solution)/shard_map/ppermute | solution.py:315
  58.5 10.2 %shard_map.139 = (bf16[256,512]{1,0:T(8,128)(2,1)}, bf16[256,512]{1,0:T(8,128)(2,1)}, bf16[256,512]{1,0:T(8,128)(2,1)}, bf16[256,512]{1,0:T(8,128)(2,1)}, f32[4,...) custom-call(s32[6]{0:T(128)} %stack.34.place_ref, ...), custom_call_target="tpu_custom_call" | custom-call | flops 12000000000 | bytes 5111808 | tf_op jit(solution)/shard_map/pallas_call | solution.py:31
  69.4 1.9 %shard_map.140 = f32[16,96,128]{2,1,0:T(8,128)} custom-call(s32[6]{0:T(128)} %stack.34.place_ref, f32[4,104,128]{2,1,0:T(8,128)} %copy-done.2), custom_call_target="tpu_custom_call" | custom-call | tf_op jit(solution)/shard_map/pallas_call | solution.py:31
  71.3 14.0 %all-to-all-start.2 = ((f32[16,96,128]{2,1,0:T(8,128)}), f32[16,96,128]{2,1,0:T(8,128)S(1)}, u32[]{:S(2)}, u32[]{:S(2)}) async-start(f32[16,96,128]{2,1,0:T(8,128)} %shard_map.140), calls=%async_computation.2 | async-start | bytes 1572864 | tf_op jit(solution)/shard_map/all_to_all | solution.py:328
  85.4 1.5 %collective-permute-start.10 = (bf16[4,256,128]{2,1,0:T(8,128)(2,1)S(1)}, bf16[4,256,128]{2,1,0:T(8,128)(2,1)S(1)}, u32[]{:S(2)}, u32[]{:S(2)}) collective-permute-start(bf16[4,256,128]{2,1,0:T(8,128)(2,1)S(1)} %copy-done.23), channel_id=1, source_target_pairs={{0,1},{1,0},{2,3},{3,2},{4,5},{5,4},{6,7},{7,6},{8,9},{9,8},{10,11... | collective-permute-start | bytes 786440 | tf_op jit(solution)/shard_map/ppermute | solution.py:321
  86.9 2.3 %collective-permute-start.11 = (bf16[256,512]{1,0:T(8,128)(2,1)S(1)}, bf16[256,512]{1,0:T(8,128)(2,1)S(1)}, u32[]{:S(2)}, u32[]{:S(2)}) collective-permute-start(bf16[256,512]{1,0:T(8,128)(2,1)S(1)} %copy-done.22), channel_id=1, source_target_pairs={{0,6},{1,7},{2,0},{3,1},{4,2},{5,3},{6,4},{7,5},{8,14},{9,15},{10,... | collective-permute-start | bytes 786440 | tf_op jit(solution)/shard_map/ppermute | solution.py:315
  91.0 8.9 %shard_map.141 = (bf16[256,512]{1,0:T(8,128)(2,1)}, bf16[256,512]{1,0:T(8,128)(2,1)}, bf16[256,512]{1,0:T(8,128)(2,1)}, bf16[256,512]{1,0:T(8,128)(2,1)}, f32[4,...) custom-call(s32[6]{0:T(128)} %stack.34.place_ref, bf16[256,1024]{1,0:T(8,128)(2,1)} %get-tuple-element.96.refs_0_, ...), custom_call_target="tpu_custom_call" | custom-call | flops 12000000000 | bytes 5111808 | tf_op jit(solution)/shard_map/pallas_call | solution.py:31
  99.9 2.6 %collective-permute-start.7 = (bf16[256,512]{1,0:T(8,128)(2,1)}, bf16[256,512]{1,0:T(8,128)(2,1)S(1)}, u32[]{:S(2)}, u32[]{:S(2)}) collective-permute-start(bf16[256,512]{1,0:T(8,128)(2,1)} %get-tuple-element.112), channel_id=1, source_target_pairs={{0,6},{1,7},{2,0},{3,1},{4,2},{5,3},{6,4},{7,5},{8,14},{9,15},{10,... | collective-permute-start | bytes 786440 | tf_op jit(solution)/shard_map/ppermute | solution.py:315
  102.5 7.8 %collective-permute-done.10.dv_far = bf16[4,256,128]{2,1,0:T(8,128)(2,1)S(1)} collective-permute-done((bf16[4,256,128]{2,1,0:T(8,128)(2,1)S(1)}, bf16[4,256,128]{2,1,0:T(8,128)(2,1)S(1)}, u32[]{:S(2)}, u32[]{:S(2)}) %collective-permute-start.10) | collective-permute-done | bytes 262176 | tf_op jit(solution)/shard_map/ppermute | solution.py:321
  110.2 2.3 %collective-permute-start.8 = (bf16[256,512]{1,0:T(8,128)(2,1)}, bf16[256,512]{1,0:T(8,128)(2,1)S(1)}, u32[]{:S(2)}, u32[]{:S(2)}) collective-permute-start(bf16[256,512]{1,0:T(8,128)(2,1)} %get-tuple-element.113), channel_id=1, source_target_pairs={{0,4},{1,5},{2,6},{3,7},{4,0},{5,1},{6,2},{7,3},{8,12},{9,13},{10,... | collective-permute-start | bytes 786440 | tf_op jit(solution)/shard_map/ppermute | solution.py:315
  112.5 1.7 %collective-permute-start.9 = (bf16[256,512]{1,0:T(8,128)(2,1)}, bf16[256,512]{1,0:T(8,128)(2,1)S(1)}, u32[]{:S(2)}, u32[]{:S(2)}) collective-permute-start(bf16[256,512]{1,0:T(8,128)(2,1)} %get-tuple-element.114), channel_id=1, source_target_pairs={{0,2},{1,3},{2,4},{3,5},{4,6},{5,7},{6,0},{7,1},{8,10},{9,11},{10,... | collective-permute-start | bytes 786440 | tf_op jit(solution)/shard_map/ppermute | solution.py:315
  114.9 3.8 %collective-permute-start.14 = (bf16[4,256,128]{2,1,0:T(8,128)(2,1)}, bf16[4,256,128]{2,1,0:T(8,128)(2,1)S(1)}, u32[]{:S(2)}, u32[]{:S(2)}) collective-permute-start(bf16[4,256,128]{2,1,0:T(8,128)(2,1)} %get-tuple-element.130), channel_id=1, source_target_pairs={{0,1},{1,0},{2,3},{3,2},{4,5},{5,4},{6,7},{7,6},{8,9},{9,8},{10,11... | collective-permute-start | bytes 786440 | tf_op jit(solution)/shard_map/ppermute | solution.py:321
  118.7 2.1 %collective-permute-done.8.refs_2_ = bf16[256,512]{1,0:T(8,128)(2,1)S(1)} collective-permute-done((bf16[256,512]{1,0:T(8,128)(2,1)}, bf16[256,512]{1,0:T(8,128)(2,1)S(1)}, u32[]{:S(2)}, u32[]{:S(2)}) %collective-permute-start.8) | collective-permute-done | bytes 262176 | tf_op jit(solution)/shard_map/ppermute | solution.py:315
  120.8 2.8 %collective-permute-done.9.refs_3_ = bf16[256,512]{1,0:T(8,128)(2,1)S(1)} collective-permute-done((bf16[256,512]{1,0:T(8,128)(2,1)}, bf16[256,512]{1,0:T(8,128)(2,1)S(1)}, u32[]{:S(2)}, u32[]{:S(2)}) %collective-permute-start.9) | collective-permute-done | bytes 262176 | tf_op jit(solution)/shard_map/ppermute | solution.py:315
  123.6 2.3 %shard_map.142 = bf16[256,2048]{1,0:T(8,128)(2,1)} custom-call(s32[6]{0:T(128)} %stack.34.place_ref, bf16[256,512]{1,0:T(8,128)(2,1)} %get-tuple-element.125.refs_0_, bf16[256,512]{1,0:T(8,128)(2,1)} %copy-done.7, bf16[256,512]{1,0:T(8,128)(2,1)} %copy-done.8, bf16[256,512]{1,0:T(8,128)(2,1)} %copy-done.10), custom_call_target="tpu_custom_call" | custom-call | tf_op jit(solution)/shard_map/pallas_call | solution.py:31
  126.0 4.6 %collective-permute-done.14.dk_far = bf16[4,256,128]{2,1,0:T(8,128)(2,1)S(1)} collective-permute-done((bf16[4,256,128]{2,1,0:T(8,128)(2,1)}, bf16[4,256,128]{2,1,0:T(8,128)(2,1)S(1)}, u32[]{:S(2)}, u32[]{:S(2)}) %collective-permute-start.14) | collective-permute-done | bytes 262176 | tf_op jit(solution)/shard_map/ppermute | solution.py:321
  131.2 2.2 %shard_map.143 = (bf16[256,256]{1,0:T(8,128)(2,1)}, bf16[256,256]{1,0:T(8,128)(2,1)}, bf16[256,256]{1,0:T(8,128)(2,1)}, bf16[256,256]{1,0:T(8,128)(2,1)}) custom-call(s32[6]{0:T(128)} %stack.34.place_ref, f32[4,256,128]{2,1,0:T(8,128)} %get-tuple-element.129.dk_near, bf16[4,256,128]{2,1,0:T(8,128)(2,1)} %copy-done.12, ...), custom_call_target="tpu_custom_call" | custom-call | tf_op jit(solution)/shard_map/pallas_call | solution.py:31
  133.5 3.3 %collective-permute-start.16 = (bf16[256,256]{1,0:T(8,128)(2,1)}, bf16[256,256]{1,0:T(8,128)(2,1)S(1)}, u32[]{:S(2)}, u32[]{:S(2)}) collective-permute-start(bf16[256,256]{1,0:T(8,128)(2,1)} %get-tuple-element.144), channel_id=1, source_target_pairs={{0,6},{1,7},{2,0},{3,1},{4,2},{5,3},{6,4},{7,5},{8,14},{9,15},{10,... | collective-permute-start | bytes 393224 | tf_op jit(solution)/shard_map/ppermute | solution.py:315
  137.7 2.2 %shard_map.144 = bf16[256,2048]{1,0:T(8,128)(2,1)} custom-call(s32[6]{0:T(128)} %stack.34.place_ref, bf16[256,512]{1,0:T(8,128)(2,1)} %get-tuple-element.136.refs_0_, bf16[256,512]{1,0:T(8,128)(2,1)} %copy-done.5, bf16[256,512]{1,0:T(8,128)(2,1)} %copy-done.6, bf16[256,512]{1,0:T(8,128)(2,1)} %copy-done.9), custom_call_target="tpu_custom_call" | custom-call | tf_op jit(solution)/shard_map/pallas_call | solution.py:31
  140.9 4.8 %shard_map.145 = (f32[96,4096]{1,0:T(8,128)}, f32[96,4096]{1,0:T(8,128)}) custom-call(s32[6]{0:T(128)} %stack.34.place_ref, f32[16,96,128]{2,1,0:T(8,128)} %copy-done.1, f32[16,96,128]{2,1,0:T(8,128)} %copy-done.3, f32[96,4096]{1,0:T(8,128)} %g_ref.3, f32[96,4096]{1,0:T(8,128)} %m_ref.1), custom_call_target="tpu_custom_call" | custom-call | tf_op jit(solution)/shard_map/pallas_call | solution.py:31
  147.5 2.0 %shard_map.146 = (bf16[256,512]{1,0:T(8,128)(2,1)}, bf16[256,512]{1,0:T(8,128)(2,1)}) custom-call(s32[6]{0:T(128)} %stack.34.place_ref, bf16[256,256]{1,0:T(8,128)(2,1)} %get-tuple-element.147.refs_0_, bf16[256,256]{1,0:T(8,128)(2,1)} %copy-done.13, bf16[256,256]{1,0:T(8,128)(2,1)} %copy-done.14, bf16[256,256]{1,0:T(8,128)(2,1)} %copy-done.15), custom_call_target="tpu_custom_call" | custom-call | tf_op jit(solution)/shard_map/pallas_call | solution.py:31
  (73 shorter events, 16.4 us)
Async XLA Ops:
  4.5 6.8 %collective-permute-start = (bf16[256,256]{1,0:T(8,128)(2,1)}, bf16[256,256]{1,0:T(8,128)(2,1)S(1)}, u32[]{:S(2)}, u32[]{:S(2)}) collective-permute-start(bf16[256,256]{1,0:T(8,128)(2,1)} %get-tuple-element.81), channel_id=1, source_target_pairs={{0,2},{1,3},{2,4},{3,5},{4,6},{5,7},{6,0},{7,1},{8,10},{9,11},{10,... | collective-permute-start | bytes 393224 | tf_op jit(solution)/shard_map/ppermute | solution.py:315
  6.0 9.0 %collective-permute-start.1 = (bf16[256,256]{1,0:T(8,128)(2,1)}, bf16[256,256]{1,0:T(8,128)(2,1)S(1)}, u32[]{:S(2)}, u32[]{:S(2)}) collective-permute-start(bf16[256,256]{1,0:T(8,128)(2,1)} %get-tuple-element.82), channel_id=1, source_target_pairs={{0,4},{1,5},{2,6},{3,7},{4,0},{5,1},{6,2},{7,3},{8,12},{9,13},{10,... | collective-permute-start | bytes 393224 | tf_op jit(solution)/shard_map/ppermute | solution.py:315
  8.7 6.2 %collective-permute-start.2 = (bf16[256,256]{1,0:T(8,128)(2,1)}, bf16[256,256]{1,0:T(8,128)(2,1)S(1)}, u32[]{:S(2)}, u32[]{:S(2)}) collective-permute-start(bf16[256,256]{1,0:T(8,128)(2,1)} %get-tuple-element.83), channel_id=1, source_target_pairs={{0,6},{1,7},{2,0},{3,1},{4,2},{5,3},{6,4},{7,5},{8,14},{9,15},{10,... | collective-permute-start | bytes 393224 | tf_op jit(solution)/shard_map/ppermute | solution.py:315
  18.5 17.6 %all-to-all-start = ((bf16[8,112,512]{2,1,0:T(8,128)(2,1)}), bf16[8,112,512]{2,1,0:T(8,128)(2,1)S(1)}, u32[]{:S(2)}, u32[]{:S(2)}) async-start(bf16[8,112,512]{2,1,0:T(8,128)(2,1)} %get-tuple-element.87), calls=%async_computation | async-start | bytes 1835008 | tf_op jit(solution)/shard_map/all_to_all | solution.py:328
  23.5 34.4 %copy-start.4 = (bf16[4,256,256]{2,1,0:T(8,128)(2,1)}, bf16[4,256,256]{2,1,0:T(8,128)(2,1)S(1)}, u32[]{:S(2)}) copy-start(bf16[4,256,256]{2,1,0:T(8,128)(2,1)S(1)} %pad_maximum_fusion.refs_4_) | copy-start | bytes 1572868
  23.5 21.8 %collective-permute-start.6 = (bf16[4,256,256]{2,1,0:T(8,128)(2,1)S(1)}, bf16[4,256,256]{2,1,0:T(8,128)(2,1)S(1)}, u32[]{:S(2)}, u32[]{:S(2)}) collective-permute-start(bf16[4,256,256]{2,1,0:T(8,128)(2,1)S(1)} %pad_maximum_fusion.refs_4_), channel_id=1, source_target_pairs={{0,1},{1,0},{2,3},{3,2},{4,5},{5,4},{6,7},{7,6},{8,9},{9,8},{10,11... | collective-permute-start | bytes 1572872 | tf_op jit(solution)/shard_map/ppermute | solution.py:321
  30.8 15.7 %collective-permute-start.3 = (bf16[256,1024]{1,0:T(8,128)(2,1)}, bf16[256,1024]{1,0:T(8,128)(2,1)S(1)}, u32[]{:S(2)}, u32[]{:S(2)}) collective-permute-start(bf16[256,1024]{1,0:T(8,128)(2,1)} %get-tuple-element.89), channel_id=1, source_target_pairs={{0,2},{1,3},{2,4},{3,5},{4,6},{5,7},{6,0},{7,1},{8,10},{9,11},{10,... | collective-permute-start | bytes 1572872 | tf_op jit(solution)/shard_map/ppermute | solution.py:315
  32.1 25.5 %collective-permute-start.4 = (bf16[256,1024]{1,0:T(8,128)(2,1)}, bf16[256,1024]{1,0:T(8,128)(2,1)S(1)}, u32[]{:S(2)}, u32[]{:S(2)}) collective-permute-start(bf16[256,1024]{1,0:T(8,128)(2,1)} %get-tuple-element.90), channel_id=1, source_target_pairs={{0,4},{1,5},{2,6},{3,7},{4,0},{5,1},{6,2},{7,3},{8,12},{9,13},{10,... | collective-permute-start | bytes 1572872 | tf_op jit(solution)/shard_map/ppermute | solution.py:315
  34.5 23.3 %collective-permute-start.5 = (bf16[256,1024]{1,0:T(8,128)(2,1)}, bf16[256,1024]{1,0:T(8,128)(2,1)}, u32[]{:S(2)}, u32[]{:S(2)}) collective-permute-start(bf16[256,1024]{1,0:T(8,128)(2,1)} %get-tuple-element.91), channel_id=1, source_target_pairs={{0,6},{1,7},{2,0},{3,1},{4,2},{5,3},{6,4},{7,5},{8,14},{9,15},{10,... | collective-permute-start | bytes 1572872 | tf_op jit(solution)/shard_map/ppermute | solution.py:315
  39.6 29.1 %all-to-all-start.1 = ((f32[4,104,128]{2,1,0:T(8,128)}), f32[4,104,128]{2,1,0:T(8,128)S(1)}, u32[]{:S(2)}, u32[]{:S(2)}) async-start(f32[4,104,128]{2,1,0:T(8,128)} %shard_map.138), calls=%async_computation.1 | async-start | bytes 425984 | tf_op jit(solution)/shard_map/all_to_all | solution.py:328
  45.3 12.6 %copy-start.17 = (bf16[4,256,256]{2,1,0:T(8,128)(2,1)}, bf16[4,256,256]{2,1,0:T(8,128)(2,1)S(1)}, u32[]{:S(2)}) copy-start(bf16[4,256,256]{2,1,0:T(8,128)(2,1)S(1)} %collective-permute-done.6.refs_5_) | copy-start | bytes 1572868
  68.7 16.7 %copy-start.23 = (bf16[4,256,128]{2,1,0:T(8,128)(2,1)S(1)}, bf16[4,256,128]{2,1,0:T(8,128)(2,1)}, u32[]{:S(2)}) copy-start(bf16[4,256,128]{2,1,0:T(8,128)(2,1)} %get-tuple-element.116) | copy-start | bytes 786436
  68.7 18.2 %copy-start.22 = (bf16[256,512]{1,0:T(8,128)(2,1)S(1)}, bf16[256,512]{1,0:T(8,128)(2,1)}, u32[]{:S(2)}) copy-start(bf16[256,512]{1,0:T(8,128)(2,1)} %get-tuple-element.118) | copy-start | bytes 786436
  68.7 20.5 %copy-start.21 = (bf16[256,512]{1,0:T(8,128)(2,1)S(1)}, bf16[256,512]{1,0:T(8,128)(2,1)}, u32[]{:S(2)}) copy-start(bf16[256,512]{1,0:T(8,128)(2,1)} %get-tuple-element.119) | copy-start | bytes 786436
  68.7 21.6 %copy-start.20 = (bf16[256,512]{1,0:T(8,128)(2,1)S(1)}, bf16[256,512]{1,0:T(8,128)(2,1)}, u32[]{:S(2)}) copy-start(bf16[256,512]{1,0:T(8,128)(2,1)} %get-tuple-element.120) | copy-start | bytes 786436
  71.3 43.6 %all-to-all-start.2 = ((f32[16,96,128]{2,1,0:T(8,128)}), f32[16,96,128]{2,1,0:T(8,128)S(1)}, u32[]{:S(2)}, u32[]{:S(2)}) async-start(f32[16,96,128]{2,1,0:T(8,128)} %shard_map.140), calls=%async_computation.2 | async-start | bytes 1572864 | tf_op jit(solution)/shard_map/all_to_all | solution.py:328
  85.4 24.8 %collective-permute-start.10 = (bf16[4,256,128]{2,1,0:T(8,128)(2,1)S(1)}, bf16[4,256,128]{2,1,0:T(8,128)(2,1)S(1)}, u32[]{:S(2)}, u32[]{:S(2)}) collective-permute-start(bf16[4,256,128]{2,1,0:T(8,128)(2,1)S(1)} %copy-done.23), channel_id=1, source_target_pairs={{0,1},{1,0},{2,3},{3,2},{4,5},{5,4},{6,7},{7,6},{8,9},{9,8},{10,11... | collective-permute-start | bytes 786440 | tf_op jit(solution)/shard_map/ppermute | solution.py:321
  86.9 25.6 %collective-permute-start.11 = (bf16[256,512]{1,0:T(8,128)(2,1)S(1)}, bf16[256,512]{1,0:T(8,128)(2,1)S(1)}, u32[]{:S(2)}, u32[]{:S(2)}) collective-permute-start(bf16[256,512]{1,0:T(8,128)(2,1)S(1)} %copy-done.22), channel_id=1, source_target_pairs={{0,6},{1,7},{2,0},{3,1},{4,2},{5,3},{6,4},{7,5},{8,14},{9,15},{10,... | collective-permute-start | bytes 786440 | tf_op jit(solution)/shard_map/ppermute | solution.py:315
  89.2 25.0 %collective-permute-start.12 = (bf16[256,512]{1,0:T(8,128)(2,1)S(1)}, bf16[256,512]{1,0:T(8,128)(2,1)S(1)}, u32[]{:S(2)}, u32[]{:S(2)}) collective-permute-start(bf16[256,512]{1,0:T(8,128)(2,1)S(1)} %copy-done.21), channel_id=1, source_target_pairs={{0,4},{1,5},{2,6},{3,7},{4,0},{5,1},{6,2},{7,3},{8,12},{9,13},{10,... | collective-permute-start | bytes 786440 | tf_op jit(solution)/shard_map/ppermute | solution.py:315
  90.3 23.9 %collective-permute-start.13 = (bf16[256,512]{1,0:T(8,128)(2,1)S(1)}, bf16[256,512]{1,0:T(8,128)(2,1)S(1)}, u32[]{:S(2)}, u32[]{:S(2)}) collective-permute-start(bf16[256,512]{1,0:T(8,128)(2,1)S(1)} %copy-done.20), channel_id=1, source_target_pairs={{0,2},{1,3},{2,4},{3,5},{4,6},{5,7},{6,0},{7,1},{8,10},{9,11},{10,... | collective-permute-start | bytes 786440 | tf_op jit(solution)/shard_map/ppermute | solution.py:315
  99.9 18.9 %collective-permute-start.7 = (bf16[256,512]{1,0:T(8,128)(2,1)}, bf16[256,512]{1,0:T(8,128)(2,1)S(1)}, u32[]{:S(2)}, u32[]{:S(2)}) collective-permute-start(bf16[256,512]{1,0:T(8,128)(2,1)} %get-tuple-element.112), channel_id=1, source_target_pairs={{0,6},{1,7},{2,0},{3,1},{4,2},{5,3},{6,4},{7,5},{8,14},{9,15},{10,... | collective-permute-start | bytes 786440 | tf_op jit(solution)/shard_map/ppermute | solution.py:315
  110.2 20.3 %copy-start.11 = (bf16[4,256,128]{2,1,0:T(8,128)(2,1)}, bf16[4,256,128]{2,1,0:T(8,128)(2,1)S(1)}, u32[]{:S(2)}) copy-start(bf16[4,256,128]{2,1,0:T(8,128)(2,1)S(1)} %collective-permute-done.10.dv_far) | copy-start | bytes 786436
  110.2 10.6 %collective-permute-start.8 = (bf16[256,512]{1,0:T(8,128)(2,1)}, bf16[256,512]{1,0:T(8,128)(2,1)S(1)}, u32[]{:S(2)}, u32[]{:S(2)}) collective-permute-start(bf16[256,512]{1,0:T(8,128)(2,1)} %get-tuple-element.113), channel_id=1, source_target_pairs={{0,4},{1,5},{2,6},{3,7},{4,0},{5,1},{6,2},{7,3},{8,12},{9,13},{10,... | collective-permute-start | bytes 786440 | tf_op jit(solution)/shard_map/ppermute | solution.py:315
  112.5 11.1 %collective-permute-start.9 = (bf16[256,512]{1,0:T(8,128)(2,1)}, bf16[256,512]{1,0:T(8,128)(2,1)S(1)}, u32[]{:S(2)}, u32[]{:S(2)}) collective-permute-start(bf16[256,512]{1,0:T(8,128)(2,1)} %get-tuple-element.114), channel_id=1, source_target_pairs={{0,2},{1,3},{2,4},{3,5},{4,6},{5,7},{6,0},{7,1},{8,10},{9,11},{10,... | collective-permute-start | bytes 786440 | tf_op jit(solution)/shard_map/ppermute | solution.py:315
  114.9 18.5 %copy-start.1 = (f32[16,96,128]{2,1,0:T(8,128)}, f32[16,96,128]{2,1,0:T(8,128)S(1)}, u32[]{:S(2)}) copy-start(f32[16,96,128]{2,1,0:T(8,128)S(1)} %all-to-all-done.2.near_ref) | copy-start | bytes 2359300
  114.9 15.6 %collective-permute-start.14 = (bf16[4,256,128]{2,1,0:T(8,128)(2,1)}, bf16[4,256,128]{2,1,0:T(8,128)(2,1)S(1)}, u32[]{:S(2)}, u32[]{:S(2)}) collective-permute-start(bf16[4,256,128]{2,1,0:T(8,128)(2,1)} %get-tuple-element.130), channel_id=1, source_target_pairs={{0,1},{1,0},{2,3},{3,2},{4,5},{5,4},{6,7},{7,6},{8,9},{9,8},{10,11... | collective-permute-start | bytes 786440 | tf_op jit(solution)/shard_map/ppermute | solution.py:321
  118.7 14.6 %copy-start.5 = (bf16[256,512]{1,0:T(8,128)(2,1)}, bf16[256,512]{1,0:T(8,128)(2,1)S(1)}, u32[]{:S(2)}) copy-start(bf16[256,512]{1,0:T(8,128)(2,1)S(1)} %collective-permute-done.7.refs_1_) | copy-start | bytes 786436
  120.8 12.6 %copy-start.6 = (bf16[256,512]{1,0:T(8,128)(2,1)}, bf16[256,512]{1,0:T(8,128)(2,1)S(1)}, u32[]{:S(2)}) copy-start(bf16[256,512]{1,0:T(8,128)(2,1)S(1)} %collective-permute-done.8.refs_2_) | copy-start | bytes 786436
  133.4 6.6 %collective-permute-start.15 = (f32[16,96,128]{2,1,0:T(8,128)S(1)}, f32[16,96,128]{2,1,0:T(8,128)S(1)}, u32[]{:S(2)}, u32[]{:S(2)}) collective-permute-start(f32[16,96,128]{2,1,0:T(8,128)S(1)} %all-to-all-done.2.near_ref), channel_id=1, source_target_pairs={{0,8},{8,0},{16,24},{24,16},{32,40},{40,32},{48,56},{56,48},{64,72... | collective-permute-start | bytes 2359304 | tf_op jit(solution)/shard_map/ppermute | solution.py:360
  133.5 12.1 %collective-permute-start.16 = (bf16[256,256]{1,0:T(8,128)(2,1)}, bf16[256,256]{1,0:T(8,128)(2,1)S(1)}, u32[]{:S(2)}, u32[]{:S(2)}) collective-permute-start(bf16[256,256]{1,0:T(8,128)(2,1)} %get-tuple-element.144), channel_id=1, source_target_pairs={{0,6},{1,7},{2,0},{3,1},{4,2},{5,3},{6,4},{7,5},{8,14},{9,15},{10,... | collective-permute-start | bytes 393224 | tf_op jit(solution)/shard_map/ppermute | solution.py:315
  136.8 8.9 %collective-permute-start.17 = (bf16[256,256]{1,0:T(8,128)(2,1)}, bf16[256,256]{1,0:T(8,128)(2,1)S(1)}, u32[]{:S(2)}, u32[]{:S(2)}) collective-permute-start(bf16[256,256]{1,0:T(8,128)(2,1)} %get-tuple-element.145), channel_id=1, source_target_pairs={{0,4},{1,5},{2,6},{3,7},{4,0},{5,1},{6,2},{7,3},{8,12},{9,13},{10,... | collective-permute-start | bytes 393224 | tf_op jit(solution)/shard_map/ppermute | solution.py:315
  137.5 9.4 %collective-permute-start.18 = (bf16[256,256]{1,0:T(8,128)(2,1)}, bf16[256,256]{1,0:T(8,128)(2,1)S(1)}, u32[]{:S(2)}, u32[]{:S(2)}) collective-permute-start(bf16[256,256]{1,0:T(8,128)(2,1)} %get-tuple-element.146), channel_id=1, source_target_pairs={{0,2},{1,3},{2,4},{3,5},{4,6},{5,7},{6,0},{7,1},{8,10},{9,11},{10,... | collective-permute-start | bytes 393224 | tf_op jit(solution)/shard_map/ppermute | solution.py:315
  (14 other events, 63.2 us)

commit v4 on v3

--- a/solution.py
+++ b/solution.py
@@ -21,7 +21,7 @@
 bf16 = jnp.bfloat16
 
 
-def call(kernel, place, ins, outs, scratch=(), flops=0, exps=0, vmem=58):
+def call(kernel, place, ins, outs, scratch=(), flops=0, exps=0, vmem=63):
     def whole(a):
         zeros = (0,) * len(a.shape)
         return pl.BlockSpec(a.shape, lambda: zeros)
@@ -204,7 +204,7 @@
         [((rows, COLS), bf16)] * groups + [near_part, far_part, ((groups, 8, wide), f32)],
         [((window, wide), f32), ((HEAD, wide), bf16), ((HEAD, wide), bf16), ((wide, HEAD), bf16), ((HEAD, window), bf16),
          ((window, 2 * HEAD), bf16), ((window, HEAD), f32), ((HEAD, wide), f32)],
-        flops=12 * 10**9, exps=10**7, vmem=58)
+        flops=12 * 10**9, exps=10**7, vmem=63)
 
 
 def backward_call(place, blocks, near, far, stat):
@@ -216,7 +216,7 @@
         [((rows, COLS), bf16)] * groups + [near_part, far_part],
         [((HEAD, wide), bf16), ((HEAD, wide), bf16), ((wide, HEAD), bf16), ((HEAD, window), bf16), ((HEAD, wide), f32),
          ((window, 2 * HEAD), bf16), ((window, HEAD), f32)],
-        flops=12 * 10**9, exps=10**7, vmem=58)
+        flops=12 * 10**9, exps=10**7, vmem=63)
 
 
 def pack_pairs_kernel(place_ref, a_ref, b_ref, *out_refs):
@@ -296,7 +296,7 @@
     count, _, width = near_ref.shape
     for c, ref in ((place_ref[4], near_ref), (1 - place_ref[4], far_ref)):
         for k in range(count):
-            z, y = divmod(k, 4)
+            y, z = divmod(k, 4)
             span = lanes((2 * y + c) * 4 + z, width)
             pseudo = ref[k]
             moment = outer_momentum * m_ref[:, span] + pseudo
@@ -322,7 +322,7 @@
 
     over_y_core = [[8 * z + i for i in range(8)] for z in range(4)]
     over_z = [[8 * z + i for z in range(4)] for i in range(8)]
-    over_z_y = [[8 * z + 2 * y + c for z in range(4) for y in range(4)] for c in range(2)]
+    over_y = [[8 * z + 2 * y + c for y in range(4)] for z in range(4) for c in range(2)]
 
     def spread(x, groups):
         return lax.all_to_all(x, "island", 0, 0, axis_index_groups=groups, tiled=True)
@@ -344,11 +344,13 @@
     v_far, drift, context, stat = lax.optimization_barrier((v_far, drift, context, stat))
     v_got = across(v_far)
     context = back(context)
-    pseudo, = call(theta_mean_kernel, place, [drift], [((16, frag_rows, piece), f32)])
+    pseudo, = call(theta_mean_kernel, place, [drift], [((4, frag_rows, piece), f32)])
     stat = after(pseudo, stat)
-    pseudo = spread(pseudo, over_z_y)
+    pseudo = spread(pseudo, over_z)
     *d_queries, k_near, k_far = backward_call(place, blocks, near, far, stat)
     k_far, v_got, context, pseudo = lax.optimization_barrier((k_far, v_got, context, pseudo))
+    pseudo = jnp.broadcast_to(pseudo, (4, 4, frag_rows, piece)).reshape(16, frag_rows, piece)
+    pseudo = spread(pseudo, over_y)
     k_got = across(k_far)
     d_queries = back(d_queries)
     context = after(d_queries, context)

time: 152 us -> 146 us (0.961)
  the two profiles are of different devices: /device:TPU:16 before, /device:TPU:105 now
where the time goes in v4:
time: 146 us
  Pallas kernels  57 us (39%)
  starting transfers between devices  51.1 us (35%)
  waiting for transfers between devices  30.3 us (21%)
  local copies, waits for them, and re-layouts  3.3 us (2%)
  between operations  2.09 us (1%)
  other arithmetic  1.89 us (1%)
    pallas_call x11, Pallas kernels, call(): pl.pallas_call(kernel, in_specs=[pl.BlockSpec(memory_space=pltpu.SMEM)] +...  57 us
    ppermute x15, waiting for transfers between devices, along(): lax.ppermute(x, 'fsdp', [(i, (i + 2 * r) % ranks) for i in range(ranks)])  22.2 us
    ppermute x15, starting transfers between devices, along(): lax.ppermute(x, 'fsdp', [(i, (i + 2 * r) % ranks) for i in range(ranks)])  20.8 us
    all_to_all x4, starting transfers between devices, spread(): lax.all_to_all(x, 'island', 0, 0, axis_index_groups=groups, tiled=True)  19.5 us
    ppermute x3, starting transfers between devices, across(): return lax.ppermute(x, 'fsdp', [(i, i ^ 1) for i in range(ranks)])  9.59 us
    ppermute x3, waiting for transfers between devices, across(): return lax.ppermute(x, 'fsdp', [(i, i ^ 1) for i in range(ranks)])  5.92 us
  transfers between devices with their start and end apart: 23, of which 10 were waited for; matrix products, arithmetic and copies ran while one was open for 1% of the time, Pallas kernels for 31%

profile of v4, /device:TPU:105, one launch (start us, length us, event | category | flops | bytes accessed | tf_op | source)
XLA Modules:
  0.0 145.7 jit_solution(9798503171259900520)
XLA Ops:
  2.6 1.9 %shard_map.136 = (bf16[256,256]{1,0:T(8,128)(2,1)}, bf16[256,256]{1,0:T(8,128)(2,1)}, bf16[256,256]{1,0:T(8,128)(2,1)}, bf16[256,256]{1,0:T(8,128)(2,1)}) custom-call(s32[6]{0:T(128)} %stack.34.place_ref, bf16[256,512]{1,0:T(8,128)(2,1)} %bitcast.23, bf16[256,512]{1,0:T(8,128)(2,1)} %bitcast.24), custom_call_target="tpu_custom_call" | custom-call | tf_op jit(solution)/shard_map/pallas_call | solution.py:31
  5.7 2.5 %collective-permute-start.1 = (bf16[256,256]{1,0:T(8,128)(2,1)}, bf16[256,256]{1,0:T(8,128)(2,1)}, u32[]{:S(2)}, u32[]{:S(2)}) collective-permute-start(bf16[256,256]{1,0:T(8,128)(2,1)} %get-tuple-element.82), channel_id=1, source_target_pairs={{0,4},{1,5},{2,6},{3,7},{4,0},{5,1},{6,2},{7,3},{8,12},{9,13},{10,... | collective-permute-start | bytes 393224 | tf_op jit(solution)/shard_map/ppermute | solution.py:315
  10.4 3.8 %collective-permute-done.1 = bf16[256,256]{1,0:T(8,128)(2,1)} collective-permute-done((bf16[256,256]{1,0:T(8,128)(2,1)}, bf16[256,256]{1,0:T(8,128)(2,1)}, u32[]{:S(2)}, u32[]{:S(2)}) %collective-permute-start.1) | collective-permute-done | bytes 131104 | tf_op jit(solution)/shard_map/ppermute | solution.py:315
  14.2 3.6 %shard_map.137 = (bf16[256,1024]{1,0:T(8,128)(2,1)}, bf16[256,1024]{1,0:T(8,128)(2,1)}, bf16[256,1024]{1,0:T(8,128)(2,1)}, bf16[256,1024]{1,0:T(8,128)(2,1)}, bf16[8,112,512]{2,1,0:T(8,128)(2,1)}) custom-call(s32[6]{0:T(128)} %stack.34.place_ref, bf16[256,2048]{1,0:T(8,128)(2,1)} %bitcast.18, bf16[256,2048]{1,0:T(8,128)(2,1)} %bitcast.19, ...), custom_call_target="tpu_custom_call" | custom-call | tf_op jit(solution)/shard_map/pallas_call | solution.py:31
  17.7 6.2 %all-to-all-start = ((bf16[8,112,512]{2,1,0:T(8,128)(2,1)}), bf16[8,112,512]{2,1,0:T(8,128)(2,1)S(1)}, u32[]{:S(2)}, u32[]{:S(2)}) async-start(bf16[8,112,512]{2,1,0:T(8,128)(2,1)} %get-tuple-element.87), calls=%async_computation | async-start | bytes 1835008 | tf_op jit(solution)/shard_map/all_to_all | solution.py:328
  24.0 1.9 %pad_maximum_fusion.refs_4_ = bf16[4,256,256]{2,1,0:T(8,128)(2,1)} fusion(bf16[1,256,256]{2,1,0:T(8,128)(2,1)} %bitcast.12, bf16[1,256,256]{2,1,0:T(8,128)(2,1)} %bitcast.11, bf16[1,256,256]{2,1,0:T(8,128)(2,1)} %bitcast.10, bf16[1,256,256]{2,1,0:T(8,128)(2,1)S(1)} %bitcast.25), kind=kLoop, calls=%fused_computation | loop fusion | flops 786432 | bytes 1048576 | tf_op jit(solution)/shard_map/stack | solution.py:334
  25.8 4.2 %collective-permute-start.6 = (bf16[4,256,256]{2,1,0:T(8,128)(2,1)}, bf16[4,256,256]{2,1,0:T(8,128)(2,1)}, u32[]{:S(2)}, u32[]{:S(2)}) collective-permute-start(bf16[4,256,256]{2,1,0:T(8,128)(2,1)} %pad_maximum_fusion.refs_4_), channel_id=1, source_target_pairs={{0,1},{1,0},{2,3},{3,2},{4,5},{5,4},{6,7},{7,6},{8,9},{9,8},{10,11... | collective-permute-start | bytes 1572872 | tf_op jit(solution)/shard_map/ppermute | solution.py:321
  31.1 2.1 %collective-permute-start.4 = (bf16[256,1024]{1,0:T(8,128)(2,1)}, bf16[256,1024]{1,0:T(8,128)(2,1)}, u32[]{:S(2)}, u32[]{:S(2)}) collective-permute-start(bf16[256,1024]{1,0:T(8,128)(2,1)} %get-tuple-element.90), channel_id=1, source_target_pairs={{0,4},{1,5},{2,6},{3,7},{4,0},{5,1},{6,2},{7,3},{8,12},{9,13},{10,... | collective-permute-start | bytes 1572872 | tf_op jit(solution)/shard_map/ppermute | solution.py:315
  33.2 1.3 collective-permute-start.5
  34.5 2.1 %all-to-all-done.in_ref = bf16[8,112,512]{2,1,0:T(8,128)(2,1)S(1)} async-done(((bf16[8,112,512]{2,1,0:T(8,128)(2,1)}), bf16[8,112,512]{2,1,0:T(8,128)(2,1)S(1)}, u32[]{:S(2)}, u32[]{:S(2)}) %all-to-all-start) | async-done | bytes 917536 | tf_op jit(solution)/shard_map/all_to_all | solution.py:328
  37.6 2.6 %shard_map.138 = f32[4,104,128]{2,1,0:T(8,128)} custom-call(s32[6]{0:T(128)} %stack.34.place_ref, f32[96,4096]{1,0:T(8,128)} %g_ref.3, bf16[8,112,512]{2,1,0:T(8,128)(2,1)} %copy-done), custom_call_target="tpu_custom_call" | custom-call | tf_op jit(solution)/shard_map/pallas_call | solution.py:31
  40.2 4.5 %all-to-all-start.1 = ((f32[4,104,128]{2,1,0:T(8,128)}), f32[4,104,128]{2,1,0:T(8,128)S(1)}, u32[]{:S(2)}, u32[]{:S(2)}) async-start(f32[4,104,128]{2,1,0:T(8,128)} %shard_map.138), calls=%async_computation.1 | async-start | bytes 425984 | tf_op jit(solution)/shard_map/all_to_all | solution.py:328
  44.7 4.5 %collective-permute-done.6.refs_5_ = bf16[4,256,256]{2,1,0:T(8,128)(2,1)} collective-permute-done((bf16[4,256,256]{2,1,0:T(8,128)(2,1)}, bf16[4,256,256]{2,1,0:T(8,128)(2,1)}, u32[]{:S(2)}, u32[]{:S(2)}) %collective-permute-start.6) | collective-permute-done | bytes 524320 | tf_op jit(solution)/shard_map/ppermute | solution.py:321
  49.2 6.9 %collective-permute-done.4.refs_2_ = bf16[256,1024]{1,0:T(8,128)(2,1)} collective-permute-done((bf16[256,1024]{1,0:T(8,128)(2,1)}, bf16[256,1024]{1,0:T(8,128)(2,1)}, u32[]{:S(2)}, u32[]{:S(2)}) %collective-permute-start.4) | collective-permute-done | bytes 524320 | tf_op jit(solution)/shard_map/ppermute | solution.py:315
  56.2 18.1 %shard_map.139 = (bf16[256,512]{1,0:T(8,128)(2,1)}, bf16[256,512]{1,0:T(8,128)(2,1)}, bf16[256,512]{1,0:T(8,128)(2,1)}, bf16[256,512]{1,0:T(8,128)(2,1)}, f32[4,...) custom-call(s32[6]{0:T(128)} %stack.34.place_ref, ...), custom_call_target="tpu_custom_call" | custom-call | flops 12000000000 | bytes 5111808 | tf_op jit(solution)/shard_map/pallas_call | solution.py:31
  75.0 1.7 %shard_map.140 = f32[4,96,128]{2,1,0:T(8,128)} custom-call(s32[6]{0:T(128)} %stack.34.place_ref, f32[4,104,128]{2,1,0:T(8,128)} %copy-done.2), custom_call_target="tpu_custom_call" | custom-call | tf_op jit(solution)/shard_map/pallas_call | solution.py:31
  76.7 4.5 %all-to-all-start.2 = ((f32[4,96,128]{2,1,0:T(8,128)}), f32[4,96,128]{2,1,0:T(8,128)S(1)}, u32[]{:S(2)}, u32[]{:S(2)}) async-start(f32[4,96,128]{2,1,0:T(8,128)} %shard_map.140), calls=%async_computation.2 | async-start | bytes 393216 | tf_op jit(solution)/shard_map/all_to_all | solution.py:328
  82.3 3.4 %collective-permute-start.11 = (bf16[256,512]{1,0:T(8,128)(2,1)}, bf16[256,512]{1,0:T(8,128)(2,1)S(1)}, u32[]{:S(2)}, u32[]{:S(2)}) collective-permute-start(bf16[256,512]{1,0:T(8,128)(2,1)} %get-tuple-element.118), channel_id=1, source_target_pairs={{0,6},{1,7},{2,0},{3,1},{4,2},{5,3},{6,4},{7,5},{8,14},{9,15},{10,... | collective-permute-start | bytes 786440 | tf_op jit(solution)/shard_map/ppermute | solution.py:315
  86.3 15.5 %shard_map.141 = (bf16[256,512]{1,0:T(8,128)(2,1)}, bf16[256,512]{1,0:T(8,128)(2,1)}, bf16[256,512]{1,0:T(8,128)(2,1)}, bf16[256,512]{1,0:T(8,128)(2,1)}, f32[4,...) custom-call(s32[6]{0:T(128)} %stack.34.place_ref, bf16[256,1024]{1,0:T(8,128)(2,1)} %get-tuple-element.96.refs_0_, ...), custom_call_target="tpu_custom_call" | custom-call | flops 12000000000 | bytes 5111808 | tf_op jit(solution)/shard_map/pallas_call | solution.py:31
  103.0 4.2 %all-to-all-start.3 = ((f32[16,96,128]{2,1,0:T(8,128)}), f32[16,96,128]{2,1,0:T(8,128)S(1)}, u32[]{:S(2)}, u32[]{:S(2)}) async-start(f32[16,96,128]{2,1,0:T(8,128)} %bitcast.14), calls=%async_computation.3 | async-start | bytes 1572864 | tf_op jit(solution)/shard_map/all_to_all | solution.py:328
  107.3 2.6 %collective-permute-start.7 = (bf16[256,512]{1,0:T(8,128)(2,1)S(1)}, bf16[256,512]{1,0:T(8,128)(2,1)}, u32[]{:S(2)}, u32[]{:S(2)}) collective-permute-start(bf16[256,512]{1,0:T(8,128)(2,1)S(1)} %copy-done.10), channel_id=1, source_target_pairs={{0,6},{1,7},{2,0},{3,1},{4,2},{5,3},{6,4},{7,5},{8,14},{9,15},{10,... | collective-permute-start | bytes 786440 | tf_op jit(solution)/shard_map/ppermute | solution.py:315
  111.1 4.2 %collective-permute-start.14 = (bf16[4,256,128]{2,1,0:T(8,128)(2,1)}, bf16[4,256,128]{2,1,0:T(8,128)(2,1)}, u32[]{:S(2)}, u32[]{:S(2)}) collective-permute-start(bf16[4,256,128]{2,1,0:T(8,128)(2,1)} %get-tuple-element.130), channel_id=1, source_target_pairs={{0,1},{1,0},{2,3},{3,2},{4,5},{5,4},{6,7},{7,6},{8,9},{9,8},{10,11... | collective-permute-start | bytes 786440 | tf_op jit(solution)/shard_map/ppermute | solution.py:321
  115.3 1.5 %collective-permute-done.8.refs_2_ = bf16[256,512]{1,0:T(8,128)(2,1)} collective-permute-done((bf16[256,512]{1,0:T(8,128)(2,1)S(1)}, bf16[256,512]{1,0:T(8,128)(2,1)}, u32[]{:S(2)}, u32[]{:S(2)}) %collective-permute-start.8) | collective-permute-done | bytes 262176 | tf_op jit(solution)/shard_map/ppermute | solution.py:315
  116.8 7.0 %collective-permute-done.9.refs_3_ = bf16[256,512]{1,0:T(8,128)(2,1)} collective-permute-done((bf16[256,512]{1,0:T(8,128)(2,1)S(1)}, bf16[256,512]{1,0:T(8,128)(2,1)}, u32[]{:S(2)}, u32[]{:S(2)}) %collective-permute-start.9) | collective-permute-done | bytes 262176 | tf_op jit(solution)/shard_map/ppermute | solution.py:315
  123.9 2.2 %shard_map.142 = bf16[256,2048]{1,0:T(8,128)(2,1)} custom-call(s32[6]{0:T(128)} %stack.34.place_ref, bf16[256,512]{1,0:T(8,128)(2,1)} %get-tuple-element.125.refs_0_, bf16[256,512]{1,0:T(8,128)(2,1)} %copy-done.3, bf16[256,512]{1,0:T(8,128)(2,1)} %copy-done.4, bf16[256,512]{1,0:T(8,128)(2,1)} %copy-done.5), custom_call_target="tpu_custom_call" | custom-call | tf_op jit(solution)/shard_map/pallas_call | solution.py:31
  126.1 1.4 collective-permute-done.14.dk_far
  127.5 2.4 %shard_map.143 = (bf16[256,256]{1,0:T(8,128)(2,1)}, bf16[256,256]{1,0:T(8,128)(2,1)}, bf16[256,256]{1,0:T(8,128)(2,1)}, bf16[256,256]{1,0:T(8,128)(2,1)}) custom-call(s32[6]{0:T(128)} %stack.34.place_ref, f32[4,256,128]{2,1,0:T(8,128)} %get-tuple-element.129.dk_near, bf16[4,256,128]{2,1,0:T(8,128)(2,1)} %collective-permute-done.14.dk_far, ...), custom_call_target="tpu_custom_call" | custom-call | tf_op jit(solution)/shard_map/pallas_call | solution.py:31
  131.2 2.5 %collective-permute-start.16 = (bf16[256,256]{1,0:T(8,128)(2,1)}, bf16[256,256]{1,0:T(8,128)(2,1)S(1)}, u32[]{:S(2)}, u32[]{:S(2)}) collective-permute-start(bf16[256,256]{1,0:T(8,128)(2,1)} %get-tuple-element.144), channel_id=1, source_target_pairs={{0,6},{1,7},{2,0},{3,1},{4,2},{5,3},{6,4},{7,5},{8,14},{9,15},{10,... | collective-permute-start | bytes 393224 | tf_op jit(solution)/shard_map/ppermute | solution.py:315
  134.9 2.2 %shard_map.144 = bf16[256,2048]{1,0:T(8,128)(2,1)} custom-call(s32[6]{0:T(128)} %stack.34.place_ref, bf16[256,512]{1,0:T(8,128)(2,1)} %get-tuple-element.136.refs_0_, bf16[256,512]{1,0:T(8,128)(2,1)} %collective-permute-done.7.refs_1_, bf16[256,512]{1,0:T(8,128)(2,1)} %collective-permute-done.8.refs_2_, bf16[256,512]{1,0:T(8,128)(2,1)} %collective-permute-done.9.refs_3_), custom_call_target="tpu_custom_call" | custom-call | tf_op jit(solution)/shard_map/pallas_call | solution.py:31
  137.1 4.7 %shard_map.145 = (f32[96,4096]{1,0:T(8,128)}, f32[96,4096]{1,0:T(8,128)}) custom-call(s32[6]{0:T(128)} %stack.34.place_ref, f32[16,96,128]{2,1,0:T(8,128)} %copy-done.1, f32[16,96,128]{2,1,0:T(8,128)} %collective-permute-done.15.far_ref, f32[96,4096]{1,0:T(8,128)} %g_ref.3, f32[96,4096]{1,0:T(8,128)} %m_ref.1), custom_call_target="tpu_custom_call" | custom-call | tf_op jit(solution)/shard_map/pallas_call | solution.py:31
  141.9 1.9 %collective-permute-done.18.refs_3_ = bf16[256,256]{1,0:T(8,128)(2,1)} collective-permute-done((bf16[256,256]{1,0:T(8,128)(2,1)}, bf16[256,256]{1,0:T(8,128)(2,1)}, u32[]{:S(2)}, u32[]{:S(2)}) %collective-permute-start.18) | collective-permute-done | bytes 131104 | tf_op jit(solution)/shard_map/ppermute | solution.py:315
  143.7 2.0 %shard_map.146 = (bf16[256,512]{1,0:T(8,128)(2,1)}, bf16[256,512]{1,0:T(8,128)(2,1)}) custom-call(s32[6]{0:T(128)} %stack.34.place_ref, bf16[256,256]{1,0:T(8,128)(2,1)} %get-tuple-element.147.refs_0_, bf16[256,256]{1,0:T(8,128)(2,1)} %copy-done.6, bf16[256,256]{1,0:T(8,128)(2,1)} %collective-permute-done.17.refs_2_, ...), custom_call_target="tpu_custom_call" | custom-call | tf_op jit(solution)/shard_map/pallas_call | solution.py:31
  (50 shorter events, 13.3 us)
Async XLA Ops:
  4.5 5.9 %collective-permute-start = (bf16[256,256]{1,0:T(8,128)(2,1)}, bf16[256,256]{1,0:T(8,128)(2,1)}, u32[]{:S(2)}, u32[]{:S(2)}) collective-permute-start(bf16[256,256]{1,0:T(8,128)(2,1)} %get-tuple-element.81), channel_id=1, source_target_pairs={{0,2},{1,3},{2,4},{3,5},{4,6},{5,7},{6,0},{7,1},{8,10},{9,11},{10,... | collective-permute-start | bytes 393224 | tf_op jit(solution)/shard_map/ppermute | solution.py:315
  5.7 8.5 %collective-permute-start.1 = (bf16[256,256]{1,0:T(8,128)(2,1)}, bf16[256,256]{1,0:T(8,128)(2,1)}, u32[]{:S(2)}, u32[]{:S(2)}) collective-permute-start(bf16[256,256]{1,0:T(8,128)(2,1)} %get-tuple-element.82), channel_id=1, source_target_pairs={{0,4},{1,5},{2,6},{3,7},{4,0},{5,1},{6,2},{7,3},{8,12},{9,13},{10,... | collective-permute-start | bytes 393224 | tf_op jit(solution)/shard_map/ppermute | solution.py:315
  8.1 6.0 %collective-permute-start.2 = (bf16[256,256]{1,0:T(8,128)(2,1)}, bf16[256,256]{1,0:T(8,128)(2,1)}, u32[]{:S(2)}, u32[]{:S(2)}) collective-permute-start(bf16[256,256]{1,0:T(8,128)(2,1)} %get-tuple-element.83), channel_id=1, source_target_pairs={{0,6},{1,7},{2,0},{3,1},{4,2},{5,3},{6,4},{7,5},{8,14},{9,15},{10,... | collective-permute-start | bytes 393224 | tf_op jit(solution)/shard_map/ppermute | solution.py:315
  17.7 6.2 %copy-start.7 = (bf16[256,256]{1,0:T(8,128)(2,1)S(1)}, bf16[256,256]{1,0:T(8,128)(2,1)}, u32[]{:S(2)}) copy-start(bf16[256,256]{1,0:T(8,128)(2,1)} %get-tuple-element.92) | copy-start | bytes 393220
  17.7 18.9 %all-to-all-start = ((bf16[8,112,512]{2,1,0:T(8,128)(2,1)}), bf16[8,112,512]{2,1,0:T(8,128)(2,1)S(1)}, u32[]{:S(2)}, u32[]{:S(2)}) async-start(bf16[8,112,512]{2,1,0:T(8,128)(2,1)} %get-tuple-element.87), calls=%async_computation | async-start | bytes 1835008 | tf_op jit(solution)/shard_map/all_to_all | solution.py:328
  25.8 23.4 %collective-permute-start.6 = (bf16[4,256,256]{2,1,0:T(8,128)(2,1)}, bf16[4,256,256]{2,1,0:T(8,128)(2,1)}, u32[]{:S(2)}, u32[]{:S(2)}) collective-permute-start(bf16[4,256,256]{2,1,0:T(8,128)(2,1)} %pad_maximum_fusion.refs_4_), channel_id=1, source_target_pairs={{0,1},{1,0},{2,3},{3,2},{4,5},{5,4},{6,7},{7,6},{8,9},{9,8},{10,11... | collective-permute-start | bytes 1572872 | tf_op jit(solution)/shard_map/ppermute | solution.py:321
  30.1 19.2 %collective-permute-start.3 = (bf16[256,1024]{1,0:T(8,128)(2,1)}, bf16[256,1024]{1,0:T(8,128)(2,1)}, u32[]{:S(2)}, u32[]{:S(2)}) collective-permute-start(bf16[256,1024]{1,0:T(8,128)(2,1)} %get-tuple-element.89), channel_id=1, source_target_pairs={{0,2},{1,3},{2,4},{3,5},{4,6},{5,7},{6,0},{7,1},{8,10},{9,11},{10,... | collective-permute-start | bytes 1572872 | tf_op jit(solution)/shard_map/ppermute | solution.py:315
  31.1 25.0 %collective-permute-start.4 = (bf16[256,1024]{1,0:T(8,128)(2,1)}, bf16[256,1024]{1,0:T(8,128)(2,1)}, u32[]{:S(2)}, u32[]{:S(2)}) collective-permute-start(bf16[256,1024]{1,0:T(8,128)(2,1)} %get-tuple-element.90), channel_id=1, source_target_pairs={{0,4},{1,5},{2,6},{3,7},{4,0},{5,1},{6,2},{7,3},{8,12},{9,13},{10,... | collective-permute-start | bytes 1572872 | tf_op jit(solution)/shard_map/ppermute | solution.py:315
  33.2 23.0 %collective-permute-start.5 = (bf16[256,1024]{1,0:T(8,128)(2,1)}, bf16[256,1024]{1,0:T(8,128)(2,1)}, u32[]{:S(2)}, u32[]{:S(2)}) collective-permute-start(bf16[256,1024]{1,0:T(8,128)(2,1)} %get-tuple-element.91), channel_id=1, source_target_pairs={{0,6},{1,7},{2,0},{3,1},{4,2},{5,3},{6,4},{7,5},{8,14},{9,15},{10,... | collective-permute-start | bytes 1572872 | tf_op jit(solution)/shard_map/ppermute | solution.py:315
  40.2 34.1 %all-to-all-start.1 = ((f32[4,104,128]{2,1,0:T(8,128)}), f32[4,104,128]{2,1,0:T(8,128)S(1)}, u32[]{:S(2)}, u32[]{:S(2)}) async-start(f32[4,104,128]{2,1,0:T(8,128)} %shard_map.138), calls=%async_computation.1 | async-start | bytes 425984 | tf_op jit(solution)/shard_map/all_to_all | solution.py:328
  76.7 25.3 %all-to-all-start.2 = ((f32[4,96,128]{2,1,0:T(8,128)}), f32[4,96,128]{2,1,0:T(8,128)S(1)}, u32[]{:S(2)}, u32[]{:S(2)}) async-start(f32[4,96,128]{2,1,0:T(8,128)} %shard_map.140), calls=%async_computation.2 | async-start | bytes 393216 | tf_op jit(solution)/shard_map/all_to_all | solution.py:328
  81.2 20.7 %collective-permute-start.10 = (bf16[4,256,128]{2,1,0:T(8,128)(2,1)}, bf16[4,256,128]{2,1,0:T(8,128)(2,1)}, u32[]{:S(2)}, u32[]{:S(2)}) collective-permute-start(bf16[4,256,128]{2,1,0:T(8,128)(2,1)} %get-tuple-element.116), channel_id=1, source_target_pairs={{0,1},{1,0},{2,3},{3,2},{4,5},{5,4},{6,7},{7,6},{8,9},{9,8},{10,11... | collective-permute-start | bytes 786440 | tf_op jit(solution)/shard_map/ppermute | solution.py:321
  82.3 19.6 %collective-permute-start.11 = (bf16[256,512]{1,0:T(8,128)(2,1)}, bf16[256,512]{1,0:T(8,128)(2,1)S(1)}, u32[]{:S(2)}, u32[]{:S(2)}) collective-permute-start(bf16[256,512]{1,0:T(8,128)(2,1)} %get-tuple-element.118), channel_id=1, source_target_pairs={{0,6},{1,7},{2,0},{3,1},{4,2},{5,3},{6,4},{7,5},{8,14},{9,15},{10,... | collective-permute-start | bytes 786440 | tf_op jit(solution)/shard_map/ppermute | solution.py:315
  85.7 16.2 %collective-permute-start.12 = (bf16[256,512]{1,0:T(8,128)(2,1)}, bf16[256,512]{1,0:T(8,128)(2,1)S(1)}, u32[]{:S(2)}, u32[]{:S(2)}) collective-permute-start(bf16[256,512]{1,0:T(8,128)(2,1)} %get-tuple-element.119), channel_id=1, source_target_pairs={{0,4},{1,5},{2,6},{3,7},{4,0},{5,1},{6,2},{7,3},{8,12},{9,13},{10,... | collective-permute-start | bytes 786440 | tf_op jit(solution)/shard_map/ppermute | solution.py:315
  86.2 15.7 %collective-permute-start.13 = (bf16[256,512]{1,0:T(8,128)(2,1)}, bf16[256,512]{1,0:T(8,128)(2,1)S(1)}, u32[]{:S(2)}, u32[]{:S(2)}) collective-permute-start(bf16[256,512]{1,0:T(8,128)(2,1)} %get-tuple-element.120), channel_id=1, source_target_pairs={{0,2},{1,3},{2,4},{3,5},{4,6},{5,7},{6,0},{7,1},{8,10},{9,11},{10,... | collective-permute-start | bytes 786440 | tf_op jit(solution)/shard_map/ppermute | solution.py:315
  101.9 5.4 %copy-start.10 = (bf16[256,512]{1,0:T(8,128)(2,1)S(1)}, bf16[256,512]{1,0:T(8,128)(2,1)}, u32[]{:S(2)}) copy-start(bf16[256,512]{1,0:T(8,128)(2,1)} %get-tuple-element.112) | copy-start | bytes 786436
  101.9 8.0 %copy-start.9 = (bf16[256,512]{1,0:T(8,128)(2,1)S(1)}, bf16[256,512]{1,0:T(8,128)(2,1)}, u32[]{:S(2)}) copy-start(bf16[256,512]{1,0:T(8,128)(2,1)} %get-tuple-element.113) | copy-start | bytes 786436
  101.9 9.2 %copy-start.8 = (bf16[256,512]{1,0:T(8,128)(2,1)S(1)}, bf16[256,512]{1,0:T(8,128)(2,1)}, u32[]{:S(2)}) copy-start(bf16[256,512]{1,0:T(8,128)(2,1)} %get-tuple-element.114) | copy-start | bytes 786436
  101.9 1.0 copy-start.3
  101.9 1.1 copy-start.4
  101.9 1.1 copy-start.5
  103.0 24.5 %all-to-all-start.3 = ((f32[16,96,128]{2,1,0:T(8,128)}), f32[16,96,128]{2,1,0:T(8,128)S(1)}, u32[]{:S(2)}, u32[]{:S(2)}) async-start(f32[16,96,128]{2,1,0:T(8,128)} %bitcast.14), calls=%async_computation.3 | async-start | bytes 1572864 | tf_op jit(solution)/shard_map/all_to_all | solution.py:328
  107.3 8.1 %collective-permute-start.7 = (bf16[256,512]{1,0:T(8,128)(2,1)S(1)}, bf16[256,512]{1,0:T(8,128)(2,1)}, u32[]{:S(2)}, u32[]{:S(2)}) collective-permute-start(bf16[256,512]{1,0:T(8,128)(2,1)S(1)} %copy-done.10), channel_id=1, source_target_pairs={{0,6},{1,7},{2,0},{3,1},{4,2},{5,3},{6,4},{7,5},{8,14},{9,15},{10,... | collective-permute-start | bytes 786440 | tf_op jit(solution)/shard_map/ppermute | solution.py:315
  109.9 6.9 %collective-permute-start.8 = (bf16[256,512]{1,0:T(8,128)(2,1)S(1)}, bf16[256,512]{1,0:T(8,128)(2,1)}, u32[]{:S(2)}, u32[]{:S(2)}) collective-permute-start(bf16[256,512]{1,0:T(8,128)(2,1)S(1)} %copy-done.9), channel_id=1, source_target_pairs={{0,4},{1,5},{2,6},{3,7},{4,0},{5,1},{6,2},{7,3},{8,12},{9,13},{10,... | collective-permute-start | bytes 786440 | tf_op jit(solution)/shard_map/ppermute | solution.py:315
  111.1 12.7 %collective-permute-start.9 = (bf16[256,512]{1,0:T(8,128)(2,1)S(1)}, bf16[256,512]{1,0:T(8,128)(2,1)}, u32[]{:S(2)}, u32[]{:S(2)}) collective-permute-start(bf16[256,512]{1,0:T(8,128)(2,1)S(1)} %copy-done.8), channel_id=1, source_target_pairs={{0,2},{1,3},{2,4},{3,5},{4,6},{5,7},{6,0},{7,1},{8,10},{9,11},{10,... | collective-permute-start | bytes 786440 | tf_op jit(solution)/shard_map/ppermute | solution.py:315
  111.1 16.4 %collective-permute-start.14 = (bf16[4,256,128]{2,1,0:T(8,128)(2,1)}, bf16[4,256,128]{2,1,0:T(8,128)(2,1)}, u32[]{:S(2)}, u32[]{:S(2)}) collective-permute-start(bf16[4,256,128]{2,1,0:T(8,128)(2,1)} %get-tuple-element.130), channel_id=1, source_target_pairs={{0,1},{1,0},{2,3},{3,2},{4,5},{5,4},{6,7},{7,6},{8,9},{9,8},{10,11... | collective-permute-start | bytes 786440 | tf_op jit(solution)/shard_map/ppermute | solution.py:321
  127.5 9.6 %copy-start.1 = (f32[16,96,128]{2,1,0:T(8,128)}, f32[16,96,128]{2,1,0:T(8,128)S(1)}, u32[]{:S(2)}) copy-start(f32[16,96,128]{2,1,0:T(8,128)S(1)} %all-to-all-done.3.near_ref) | copy-start | bytes 2359300
  130.0 7.2 %collective-permute-start.15 = (f32[16,96,128]{2,1,0:T(8,128)S(1)}, f32[16,96,128]{2,1,0:T(8,128)}, u32[]{:S(2)}, u32[]{:S(2)}) collective-permute-start(f32[16,96,128]{2,1,0:T(8,128)S(1)} %all-to-all-done.3.near_ref), channel_id=1, source_target_pairs={{0,8},{8,0},{16,24},{24,16},{32,40},{40,32},{48,56},{56,48},{64,72... | collective-permute-start | bytes 2359304 | tf_op jit(solution)/shard_map/ppermute | solution.py:362
  131.2 10.6 %collective-permute-start.16 = (bf16[256,256]{1,0:T(8,128)(2,1)}, bf16[256,256]{1,0:T(8,128)(2,1)S(1)}, u32[]{:S(2)}, u32[]{:S(2)}) collective-permute-start(bf16[256,256]{1,0:T(8,128)(2,1)} %get-tuple-element.144), channel_id=1, source_target_pairs={{0,6},{1,7},{2,0},{3,1},{4,2},{5,3},{6,4},{7,5},{8,14},{9,15},{10,... | collective-permute-start | bytes 393224 | tf_op jit(solution)/shard_map/ppermute | solution.py:315
  133.7 8.2 %collective-permute-start.17 = (bf16[256,256]{1,0:T(8,128)(2,1)}, bf16[256,256]{1,0:T(8,128)(2,1)}, u32[]{:S(2)}, u32[]{:S(2)}) collective-permute-start(bf16[256,256]{1,0:T(8,128)(2,1)} %get-tuple-element.145), channel_id=1, source_target_pairs={{0,4},{1,5},{2,6},{3,7},{4,0},{5,1},{6,2},{7,3},{8,12},{9,13},{10,... | collective-permute-start | bytes 393224 | tf_op jit(solution)/shard_map/ppermute | solution.py:315
  134.2 9.5 %collective-permute-start.18 = (bf16[256,256]{1,0:T(8,128)(2,1)}, bf16[256,256]{1,0:T(8,128)(2,1)}, u32[]{:S(2)}, u32[]{:S(2)}) collective-permute-start(bf16[256,256]{1,0:T(8,128)(2,1)} %get-tuple-element.146), channel_id=1, source_target_pairs={{0,2},{1,3},{2,4},{3,5},{4,6},{5,7},{6,0},{7,1},{8,10},{9,11},{10,... | collective-permute-start | bytes 393224 | tf_op jit(solution)/shard_map/ppermute | solution.py:315
  141.9 1.9 %copy-start.6 = (bf16[256,256]{1,0:T(8,128)(2,1)}, bf16[256,256]{1,0:T(8,128)(2,1)S(1)}, u32[]{:S(2)}) copy-start(bf16[256,256]{1,0:T(8,128)(2,1)S(1)} %collective-permute-done.16.refs_1_) | copy-start | bytes 393220
  (2 other events, 1.6 us)
